TPU v7x, 32 devices: a whole 2x2x4 slice. The times are simulated.
32 devices in a mesh: member: 4 (over y, x), dp: 8 (over z, core).
Axes of the slice: x: 2, y: 2, z: 4, core: 2. Of those that a mesh axis runs over, the one named last changes fastest.
Arguments:
- inputs: bfloat16 [2048, 64], P('dp'), may hold values from -6 to 6
- observed: float32 [64, 2048], P('member', 'dp'), may hold values from -6 to 6
- noise: bfloat16 [2, 8, 64, 2048], P(None, None, 'member', 'dp'), may hold values from -4 to 4
- w_in: float32 [8, 64, 4096], P('member', None, 'dp'), may hold values from -0.75 to 0.75
- b_in: float32 [8, 4096], P('member', 'dp'), may hold values from -3 to 3
- w_out: float32 [8, 64, 4096], P('member', None, 'dp'), may hold values from -0.09375 to 0.09375
- b_out: float32 [8, 64], P('member'), may hold values from -3 to 3
Outputs:
- new_w_in: float32 [8, 64, 4096], P('member', None, 'dp')
- new_b_in: float32 [8, 4096], P('member', 'dp')
- new_w_out: float32 [8, 64, 4096], P('member', None, 'dp')
- new_b_out: float32 [8, 64], P('member')
All inputs are finite; a program needn't handle non-finite values.
Results may differ from a plain program's by a relative error of at most 0.00056.
Values may be sent and summed in bfloat16 or wider, within the bound.
A program may use at most 64 MiB of HBM per device.

v0:
```python
import jax
import jax.numpy as jnp
from jax import lax
from jax.sharding import PartitionSpec as P

UPDATES = 2


ridge_level = 0.5


def solve_gain(gram, cross):
    eye = jnp.eye(gram.shape[0], dtype=gram.dtype)
    factor = jnp.linalg.cholesky(gram + ridge_level * eye)
    middle = lax.linalg.triangular_solve(factor, cross, left_side=True, lower=True)
    return lax.linalg.triangular_solve(factor, middle, left_side=True, lower=True, transpose_a=True)


def predict(inputs, w_in, b_in, w_out, b_out):
    shards = (
        w_in.astype(jnp.bfloat16),
        w_out.astype(jnp.bfloat16),
        b_in.astype(jnp.bfloat16)[:, None, :],
    )

    def single(item):
        weight_in, weight_out, bias_in = item
        pre = jnp.dot(inputs, weight_in, preferred_element_type=jnp.float32) + bias_in.astype(
            jnp.float32
        )
        hidden = jnp.tanh(pre).astype(jnp.bfloat16)
        return lax.dot_general(
            weight_out, hidden, (((1,), (1,)), ((), ())), preferred_element_type=jnp.float32
        )

    total = lax.map(
        single,
        (
            lax.all_gather(shards[0], "dp", axis=2, tiled=True),
            lax.all_gather(shards[1], "dp", axis=2, tiled=True),
            lax.all_gather(shards[2], "dp", axis=2, tiled=True),
        ),
    )
    return total + b_out[:, :, None]


def mix_own(own, whole, columns):
    flat = whole.reshape(whole.shape[0], -1)
    moved = lax.dot_general(
        columns, flat, (((0,), (0,)), ((), ())), precision=lax.Precision.HIGHEST
    )
    return own + moved.reshape(own.shape)


def on_device(inputs, observed, noise, w_in, b_in, w_out, b_out):
    per_device = w_in.shape[0]
    count = observed.shape[0] * lax.axis_size("member") * observed.shape[1] * lax.axis_size("dp")
    for update in range(UPDATES):
        predicted = predict(inputs, w_in, b_in, w_out, b_out)
        collected = lax.all_to_all(
            predicted.astype(jnp.bfloat16), "member", split_axis=1, concat_axis=0, tiled=True
        ).astype(predicted.dtype)
        mean_pred = jnp.mean(collected, axis=0)
        anomaly = (collected - mean_pred[None]).reshape(collected.shape[0], -1)
        misfit = (observed[None] + noise[update].astype(jnp.float32) - collected).reshape(
            collected.shape[0], -1
        )
        gram_part = lax.dot_general(
            anomaly, anomaly, (((1,), (1,)), ((), ())), precision=lax.Precision.HIGHEST
        )
        cross_part = lax.dot_general(
            anomaly, misfit, (((1,), (1,)), ((), ())), precision=lax.Precision.HIGHEST
        )
        gram, cross = lax.psum((gram_part, cross_part), ("member", "dp"))
        gain = solve_gain(gram / count, cross / count)
        whole_in, whole_bias, whole_out, whole_bout = (
            lax.all_gather(w_in, "member", axis=0, tiled=True),
            lax.all_gather(b_in, "member", axis=0, tiled=True),
            lax.all_gather(w_out, "member", axis=0, tiled=True),
            lax.all_gather(b_out, "member", axis=0, tiled=True),
        )
        first = lax.axis_index("member") * per_device
        columns = lax.dynamic_slice_in_dim(gain, first, per_device, 1)
        w_in = mix_own(w_in, whole_in, columns)
        b_in = mix_own(b_in, whole_bias, columns)
        w_out = mix_own(w_out, whole_out, columns)
        b_out = mix_own(b_out, whole_bout, columns)
    return (w_in, b_in, w_out, b_out)


def solution(mesh):
    placed = (
        P("dp", None),
        P("member", "dp"),
        P(None, None, "member", "dp"),
        P("member", None, "dp"),
        P("member", "dp"),
        P("member", None, "dp"),
        P("member", None),
    )
    return jax.shard_map(
        on_device,
        mesh=mesh,
        in_specs=placed,
        out_specs=(
            P("member", None, "dp"),
            P("member", "dp"),
            P("member", None, "dp"),
            P("member", None),
        ),
        check_vma=False,
    )
```

profile of v0, /device:TPU:0, one launch (start us, length us, event | category | flops | bytes accessed | tf_op | source)
XLA Modules:
  0.0 256.2 jit_solution(9989042823797466848)
XLA Ops:
  7.2 1.6 convert_element_type.118
  8.9 1.6 convert_element_type.119
  10.6 0.7 all-gather.21.cloned.1.call-update
  11.3 14.5 %all-gather = bf16[2,4096]{1,0:T(2,128)(2,1)S(1)} all-gather(bf16[2,512]{1,0:T(2,128)(2,1)S(1)} %convert_element_type.120), channel_id=2, replica_groups=mesh['member'=4,'dp'=8] {'dp'}, dimensions={1}, use_global_device_ids=true | all-gather | bytes 18432 | tf_op jit(solution)/shard_map/all_gather | solution.py:41
  25.8 9.2 %all-gather.15.cloned.1.call-done = bf16[2,64,4096]{2,1,0:T(8,128)(2,1)} async-done(((bf16[2,64,512]{2,1,0:T(8,128)(2,1)}), bf16[2,64,4096]{2,1,0:T(8,128)(2,1)}) %all-gather.15.cloned.1.call-update) | async-done | bytes 1048592 | tf_op jit(solution)/shard_map/all_gather | solution.py:40
  35.0 24.0 %all-gather.17.cloned.1.call-done = bf16[2,64,4096]{2,1,0:T(8,128)(2,1)} async-done(((bf16[2,64,512]{2,1,0:T(8,128)(2,1)}), bf16[2,64,4096]{2,1,0:T(8,128)(2,1)}) %all-gather.17.cloned.1.call-update) | async-done | bytes 1048592 | tf_op jit(solution)/shard_map/all_gather | solution.py:39
  59.0 5.3 %while.20 = (s32[]{:T(128)}, f32[2,64,256]{2,1,0:T(8,128)S(1)}, bf16[2,64,4096]{2,1,0:T(8,128)(2,1)}, bf16[2,64,4096]{2,1,0:T(8,128)(2,1)}, bf16[256,64]{0,1:T(8...) while((s32[]{:T(128)}, f32[2,64,256]{2,1,0:T(8,128)S(1)}, bf16[2,64,4096]{2,1,0:T(8,128)(2,1)}, ...), condition=%wide.region_1.2_spmd, body=%wide.region_0.1_spmd.sunk | while | flops 270536704 | bytes 1189457 | solution.py:36
  59.1 2.6 %fusion.92 = f32[2,64,256]{2,1,0:T(8,128)S(1)} fusion(f32[2,64,256]{2,1,0:T(8,128)S(1)} %get-tuple-element.247, s32[]{:T(128)} %get-tuple-element.246, bf16[256,64]{0,1:T(8,128)(2,1)S(1)} %get-tuple-element.257, f32[4096]{0:T(1024)S(1)} %bitcast.206, bf16[2,64,4096]{2,1,0:T(8,128)(2,1)} %get-tuple-element.256, ...), kind=kOutput, calls=%fused_computation.5.clone.1 | convolution fusion | flops 270532608 | bytes 1164800 | tf_op jit(solution)/shard_map/while/body/eval_jaxpr/dot_general | solution.py:32
  61.7 2.6 %fusion.92 = f32[2,64,256]{2,1,0:T(8,128)S(1)} fusion(f32[2,64,256]{2,1,0:T(8,128)S(1)} %get-tuple-element.247, s32[]{:T(128)} %get-tuple-element.246, bf16[256,64]{0,1:T(8,128)(2,1)S(1)} %get-tuple-element.257, f32[4096]{0:T(1024)S(1)} %bitcast.206, bf16[2,64,4096]{2,1,0:T(8,128)(2,1)} %get-tuple-element.256, ...), kind=kOutput, calls=%fused_computation.5.clone.1 | convolution fusion | flops 270532608 | bytes 1164800 | tf_op jit(solution)/shard_map/while/body/eval_jaxpr/dot_general | solution.py:32
  64.4 0.7 copy.81
  65.1 3.6 %all-to-all-start = ((bf16[2,64,256]{2,0,1:T(2,128)(2,1)}), bf16[2,64,256]{2,0,1:T(2,128)(2,1)S(1)}, u32[]{:S(2)}, u32[]{:S(2)}) async-start(bf16[2,64,256]{2,0,1:T(2,128)(2,1)} %copy.81), calls=%async_computation | async-start | bytes 131072 | tf_op jit(solution)/shard_map/all_to_all | solution.py:60
  68.8 0.6 all-gather.19.cloned.1.call-update
  69.4 4.5 %all-to-all-done = bf16[2,64,256]{2,0,1:T(2,128)(2,1)S(1)} async-done(((bf16[2,64,256]{2,0,1:T(2,128)(2,1)}), bf16[2,64,256]{2,0,1:T(2,128)(2,1)S(1)}, u32[]{:S(2)}, u32[]{:S(2)}) %all-to-all-start) | async-done | bytes 65568 | tf_op jit(solution)/shard_map/all_to_all | solution.py:60
  74.7 0.4 convolution_bitcast_fusion.2
  75.1 39.7 %all-reduce.1 = (f32[8,8]{0,1:T(8,128)S(1)}, f32[8,8]{0,1:T(8,128)S(1)}) all-reduce(f32[8,8]{0,1:T(8,128)S(1)} %convolution_bitcast_fusion.3, f32[8,8]{0,1:T(8,128)S(1)} %convolution_bitcast_fusion.2), channel_id=1, replica_groups=mesh['member'=4,'dp'=8] {'member','dp'}, use_global_device_ids=true, to_apply=%region_3.4 | all-reduce | flops 128 | bytes 1024 | tf_op jit(solution)/shard_map/psum | solution.py:74
  114.9 0.7 cholesky.44
  115.7 0.6 compare_reduce_fusion.1
  116.3 0.6 fusion.34
  117.0 0.6 custom-call.11
  118.0 3.6 %fusion.56 = (bf16[2,64,512]{2,0,1:T(2,128)(2,1)}, f32[2,64,512]{2,0,1:T(2,128)S(1)}) fusion(f32[8,8]{0,1:T(8,128)S(1)} %fusion.42, s32[]{:T(128)S(6)} %select_n.7, f32[2,64,512]{2,1,0:T(8,128)S(1)} %copy-done, f32[1,8,64,512]{3,2,1,0:T(8,128)} %bitcast.200), kind=kOutput, calls=%fused_computation.89 | convolution fusion | flops 6422528 | bytes 1704964 | tf_op jit(solution)/shard_map/dot_general | solution.py:49
  121.7 3.6 %fusion.57 = (bf16[2,64,512]{2,0,1:T(2,128)(2,1)}, f32[2,64,512]{2,0,1:T(2,128)S(1)}) fusion(f32[8,8]{0,1:T(8,128)S(1)} %fusion.42, s32[]{:T(128)S(6)} %select_n.7, f32[2,64,512]{2,1,0:T(8,128)S(1)} %copy-done.1, f32[1,8,64,512]{3,2,1,0:T(8,128)} %bitcast.201), kind=kOutput, calls=%fused_computation.90 | convolution fusion | flops 6422528 | bytes 1704964 | tf_op jit(solution)/shard_map/dot_general | solution.py:49
  125.3 8.9 %all-gather.2 = f32[4,2,512]{2,1,0:T(2,128)S(1)} all-gather(f32[1,2,512]{2,1,0:T(2,128)S(1)} %bitcast.209), channel_id=1, replica_groups=mesh['member'=4,'dp'=8] {'member'}, dimensions={0}, use_global_device_ids=true | all-gather | bytes 20480 | tf_op jit(solution)/shard_map/all_gather | solution.py:78
  134.2 7.7 %all-gather.3 = f32[4,2,64]{2,1,0:T(2,128)S(1)} all-gather(f32[1,2,64]{2,1,0:T(2,128)S(1)} %bitcast.213), channel_id=1, replica_groups=mesh['member'=4,'dp'=8] {'member'}, dimensions={0}, use_global_device_ids=true | all-gather | bytes 2560 | tf_op jit(solution)/shard_map/all_gather | solution.py:80
  141.9 0.8 copy.105
  142.8 12.7 %all-gather.1 = bf16[2,4096]{1,0:T(2,128)(2,1)S(1)} all-gather(bf16[2,512]{1,0:T(2,128)(2,1)S(1)} %get-tuple-element.163), channel_id=3, replica_groups=mesh['member'=4,'dp'=8] {'dp'}, dimensions={1}, use_global_device_ids=true | all-gather | bytes 18432 | tf_op jit(solution)/shard_map/all_gather | solution.py:41
  155.7 1.8 copy.92
  157.5 12.5 %all-gather.25.cloned.1.call-done = bf16[2,64,4096]{2,0,1:T(2,128)(2,1)} async-done(((bf16[2,64,512]{2,0,1:T(2,128)(2,1)}), bf16[2,64,4096]{2,0,1:T(2,128)(2,1)}) %all-gather.25.cloned.1.call-update) | async-done | bytes 1048592 | tf_op jit(solution)/shard_map/all_gather | solution.py:39
  170.0 1.8 copy.93
  171.9 2.9 %while.21 = (s32[]{:T(128)}, f32[2,64,256]{2,1,0:T(8,128)S(1)}, bf16[2,64,4096]{2,1,0:T(8,128)(2,1)S(1)}, bf16[2,64,4096]{2,1,0:T(8,128)(2,1)S(1)}, bf16[256,64]...) while((s32[]{:T(128)}, f32[2,64,256]{2,1,0:T(8,128)S(1)}, ...), condition=%wide.region_8.12_spmd, body=%wide.region_7.11_spmd.sunk | while | flops 270536704 | bytes 1189457 | solution.py:36
  171.9 1.4 fusion.96
  173.4 1.4 fusion.96
  174.8 0.7 copy.95
  175.5 3.3 %all-to-all-start.1 = ((bf16[2,64,256]{2,0,1:T(2,128)(2,1)}), bf16[2,64,256]{2,0,1:T(2,128)(2,1)S(1)}, u32[]{:S(2)}, u32[]{:S(2)}) async-start(bf16[2,64,256]{2,0,1:T(2,128)(2,1)} %copy.95), calls=%async_computation.1 | async-start | bytes 131072 | tf_op jit(solution)/shard_map/all_to_all | solution.py:60
  178.9 8.6 %all-gather.4 = f32[4,2,512]{2,1,0:T(2,128)S(1)} all-gather(f32[1,2,512]{2,1,0:T(2,128)S(1)} %bitcast.208), channel_id=1, replica_groups=mesh['member'=4,'dp'=8] {'member'}, dimensions={0}, use_global_device_ids=true | all-gather | bytes 20480 | tf_op jit(solution)/shard_map/all_gather | solution.py:78
  187.5 0.8 copy.104
  188.3 8.1 %all-gather.5 = f32[4,2,64]{2,1,0:T(2,128)S(1)} all-gather(f32[1,2,64]{2,1,0:T(2,128)S(1)} %bitcast.210), channel_id=1, replica_groups=mesh['member'=4,'dp'=8] {'member'}, dimensions={0}, use_global_device_ids=true | all-gather | bytes 2560 | tf_op jit(solution)/shard_map/all_gather | solution.py:80
  197.2 0.5 convolution_bitcast_fusion
  197.7 40.2 %all-reduce = (f32[8,8]{0,1:T(8,128)S(1)}, f32[8,8]{0,1:T(8,128)S(1)}) all-reduce(f32[8,8]{0,1:T(8,128)S(1)} %convolution_bitcast_fusion.1, f32[8,8]{0,1:T(8,128)S(1)} %convolution_bitcast_fusion), channel_id=1, replica_groups=mesh['member'=4,'dp'=8] {'member','dp'}, use_global_device_ids=true, to_apply=%region_10.14 | all-reduce | flops 128 | bytes 1024 | tf_op jit(solution)/shard_map/psum | solution.py:74
  237.9 0.7 cholesky.55
  238.7 0.6 compare_reduce_fusion
  239.3 0.6 fusion.35
  240.0 0.6 custom-call.13
  241.0 2.7 %convolution_add_fusion.2 = f32[2,64,512]{2,0,1:T(2,128)S(1)} fusion(f32[2,64,512]{2,0,1:T(2,128)S(1)} %get-tuple-element.160, f32[8,8]{0,1:T(8,128)S(1)} %fusion.38, s32[]{:T(128)S(6)} %select_n.7, f32[1,8,64,512]{3,2,1,0:T(8,128)} %bitcast.198), kind=kOutput, calls=%fused_computation.24 | convolution fusion | flops 6356992 | bytes 1573892 | tf_op jit(solution)/shard_map/dot_general | solution.py:49
  243.7 0.8 copy.107
  244.5 0.7 convolution_add_fusion.8
  245.2 0.7 convolution_add_fusion.6
  245.9 2.7 %convolution_add_fusion.3 = f32[2,64,512]{2,0,1:T(2,128)S(1)} fusion(f32[2,64,512]{2,0,1:T(2,128)S(1)} %get-tuple-element.162, f32[8,8]{0,1:T(8,128)S(1)} %fusion.38, s32[]{:T(128)S(6)} %select_n.7, f32[1,8,64,512]{3,2,1,0:T(8,128)} %bitcast.199), kind=kOutput, calls=%fused_computation.25 | convolution fusion | flops 6356992 | bytes 1573892 | tf_op jit(solution)/shard_map/dot_general | solution.py:49
  248.7 0.8 copy.106
  (77 shorter events, 3.5 us)
Async XLA Ops:
  7.2 4.2 %copy-start.4 = (f32[2,512]{1,0:T(2,128)S(1)}, f32[2,512]{1,0:T(2,128)}, u32[]{:S(2)}) copy-start(f32[2,512]{1,0:T(2,128)} %param.20) | copy-start | bytes 12292
  7.2 51.8 %copy-start.6 = (bf16[256,64]{0,1:T(8,128)(2,1)S(1)}, bf16[256,64]{0,1:T(8,128)(2,1)}, u32[]{:S(2)}) copy-start(bf16[256,64]{0,1:T(8,128)(2,1)} %param.16) | copy-start | bytes 98308
  7.2 27.9 %all-gather.15.cloned.1.call-start = ((), (), s32[]{:S(2)}) async-start(), calls=%async_computation.2 | async-start | bytes 1179648 | tf_op jit(solution)/shard_map/all_gather | solution.py:40
  8.9 50.1 %all-gather.17.cloned.1.call-start = ((), (), s32[]{:S(2)}) async-start(), calls=%async_computation.3 | async-start | bytes 1179648 | tf_op jit(solution)/shard_map/all_gather | solution.py:39
  10.6 107.4 %all-gather.21.cloned.1.call-start = ((), (), s32[]{:S(2)}) async-start(), calls=%async_computation.5 | async-start | bytes 1310720 | tf_op jit(solution)/shard_map/all_gather | solution.py:79
  59.0 5.3 %copy-start.5 = (f32[2,64]{1,0:T(2,128)S(1)}, f32[2,64]{1,0:T(2,128)}, u32[]{:S(2)}) copy-start(f32[2,64]{1,0:T(2,128)} %param.22) | copy-start | bytes 1540
  64.4 10.2 %copy-start.2 = (bf16[2,8,16,256]{3,2,1,0:T(8,128)(2,1)S(1)}, bf16[2,8,16,256]{3,2,1,0:T(8,128)(2,1)}, u32[]{:S(2)}) copy-start(bf16[2,8,16,256]{3,2,1,0:T(8,128)(2,1)} %param.18) | copy-start | bytes 393220
  64.4 10.2 %copy-start.3 = (f32[16,256]{1,0:T(8,128)S(1)}, f32[16,256]{1,0:T(8,128)}, u32[]{:S(2)}) copy-start(f32[16,256]{1,0:T(8,128)} %param.17) | copy-start | bytes 49156
  65.1 8.8 %all-to-all-start = ((bf16[2,64,256]{2,0,1:T(2,128)(2,1)}), bf16[2,64,256]{2,0,1:T(2,128)(2,1)S(1)}, u32[]{:S(2)}, u32[]{:S(2)}) async-start(bf16[2,64,256]{2,0,1:T(2,128)(2,1)} %copy.81), calls=%async_computation | async-start | bytes 131072 | tf_op jit(solution)/shard_map/all_to_all | solution.py:60
  68.8 52.9 %all-gather.19.cloned.1.call-start = ((), (), s32[]{:S(2)}) async-start(), calls=%async_computation.4 | async-start | bytes 1310720 | tf_op jit(solution)/shard_map/all_gather | solution.py:77
  69.3 86.4 %all-gather.23.cloned.1.call-start = ((), (), s32[]{:S(2)}) async-start(), calls=%async_computation.6 | async-start | bytes 1179648 | tf_op jit(solution)/shard_map/all_gather | solution.py:40
  74.0 44.0 %copy-start = (f32[2,64,512]{2,1,0:T(8,128)S(1)}, f32[2,64,512]{2,1,0:T(8,128)}, u32[]{:S(2)}) copy-start(f32[2,64,512]{2,1,0:T(8,128)} %param.21) | copy-start | bytes 786436
  74.7 47.0 %copy-start.1 = (f32[2,64,512]{2,1,0:T(8,128)S(1)}, f32[2,64,512]{2,1,0:T(8,128)}, u32[]{:S(2)}) copy-start(f32[2,64,512]{2,1,0:T(8,128)} %param.19) | copy-start | bytes 786436
  121.6 48.5 %all-gather.25.cloned.1.call-start = ((), (), s32[]{:S(2)}) async-start(), calls=%async_computation.7 | async-start | bytes 1179648 | tf_op jit(solution)/shard_map/all_gather | solution.py:39
  125.3 115.7 %all-gather.29.cloned.1.call-start = ((), (), s32[]{:S(2)}) async-start(), calls=%async_computation.9 | async-start | bytes 1310720 | tf_op jit(solution)/shard_map/all_gather | solution.py:79
  175.5 20.9 %all-to-all-start.1 = ((bf16[2,64,256]{2,0,1:T(2,128)(2,1)}), bf16[2,64,256]{2,0,1:T(2,128)(2,1)S(1)}, u32[]{:S(2)}, u32[]{:S(2)}) async-start(bf16[2,64,256]{2,0,1:T(2,128)(2,1)} %copy.95), calls=%async_computation.1 | async-start | bytes 131072 | tf_op jit(solution)/shard_map/all_to_all | solution.py:60
  178.8 67.1 %all-gather.27.cloned.1.call-start = ((), (), s32[]{:S(2)}) async-start(), calls=%async_computation.8 | async-start | bytes 1310720 | tf_op jit(solution)/shard_map/all_gather | solution.py:77
Sparse Core Ops, SparseCore 0:
  10.2 24.7 all-gather.14
  37.2 21.7 all-gather.16
  60.9 26.9 all-gather.20
  89.5 27.1 all-gather.18
  121.7 23.6 all-gather.22
  147.4 22.5 all-gather.24
  172.5 25.8 all-gather.28
  200.7 26.7 all-gather.26
where the time goes:
time: 257 us; the launch traced here: 256 us
  blocking collectives  140 us (54%)
  waiting for transfers between devices  51.6 us (20%)
  matrix products  24.6 us (10%)
  between operations  14.5 us (6%)
  other arithmetic  9.31 us (4%)
  local copies, waits for them, and re-layouts  8.51 us (3%)
  starting transfers between devices  7.2 us (3%)
    psum x2, blocking collectives, on_device(): gram, cross = lax.psum((gram_part, cross_part), ('member', 'dp'))  79.9 us
    all_gather x2, waiting for transfers between devices, predict(): lax.all_gather(shards[0], 'dp', axis=2, tiled=True)  36.5 us
    all_gather x2, blocking collectives, predict(): lax.all_gather(shards[2], 'dp', axis=2, tiled=True)  27.2 us
    all_gather x2, blocking collectives, on_device(): lax.all_gather(b_in, 'member', axis=0, tiled=True)  17.6 us
    all_gather x2, blocking collectives, on_device(): lax.all_gather(b_out, 'member', axis=0, tiled=True)  15.8 us
    dot_general x8, matrix products, mix_own(): lax.dot_general(columns, flat, (((0,), (0,)), ((), ())), precision=lax.Pr...  14.3 us
    all_gather x2, waiting for transfers between devices, predict(): lax.all_gather(shards[1], 'dp', axis=2, tiled=True)  9.23 us
    dot_general x4, matrix products, single(): lax.dot_general(weight_out, hidden, (((1,), (1,)), ((), ())), preferred_e...  7.96 us
  transfers between devices with their start and end apart: 10, of which 4 were waited for; matrix products, arithmetic and copies ran while one was open for 15% of the time, Pallas kernels for 0%

commit v1 on v0

v1 whole, which is shorter than its diff:
```python
import functools

import jax
import jax.numpy as jnp
from jax import lax
from jax.experimental import pallas as pl
from jax.experimental.pallas import tpu as pltpu
from jax.sharding import PartitionSpec as P

UPDATES = 2
RIDGE = 0.5
CORES = 2
MESH = pl.DeviceIdType.MESH
NT = (((1,), (1,)), ((), ()))


def kernel(
    M, Z, total,
    x_ref, obs_ref, noise_ref, w_in_ref, w_out_ref, extra_ref,
    new_in_ref, new_out_ref, new_extra_ref,
    xg, hi, lo, fresh, other, bias, staged, got, anomalies, misfits, pair, every,
    x_send, x_recv, hi_send, hi_recv, lo_send, lo_recv, w_send, w_recv,
    piece_send, piece_recv, pair_send, pair_recv, every_send, every_recv,
):
    f32, bf16 = jnp.float32, jnp.bfloat16
    m = lax.axis_index("member")
    d = lax.axis_index("dp")
    z, c = d // CORES, d % CORES
    per, F = w_in_ref.shape[0], w_in_ref.shape[1]
    O, hl = w_out_ref.shape[1], w_out_ref.shape[2]
    K = per * M
    ob = O // M
    samples = noise_ref.shape[2]
    rows = hi.shape[2]
    slots = Z * M
    me = z * M + m
    twin = (m, z * CORES + (1 - c))

    def at(dm, dz):
        return lax.rem(m + dm, M), lax.rem(z - dz + Z, Z) * CORES + c

    def send(src, dst, send_sem, recv_sem, target):
        pltpu.make_async_remote_copy(
            src_ref=src, dst_ref=dst, send_sem=send_sem, recv_sem=recv_sem,
            device_id=target, device_id_type=MESH,
        ).start()

    def settle(ref, sem):
        pltpu.make_async_copy(ref, ref, sem).wait()

    barrier = pltpu.get_barrier_semaphore()
    pl.semaphore_signal(barrier, inc=1, device_id=twin, device_id_type=MESH)

    def greet(i, carry):
        pl.semaphore_signal(
            barrier, inc=1, device_id=at(lax.rem(i, M), i // M), device_id_type=MESH
        )
        return carry

    lax.fori_loop(1, slots, greet, 0)

    for j in range(per):
        for top, part in ((0, w_in_ref[j]), (F, w_out_ref[j]), (F + O, extra_ref[j])):
            high = part.astype(bf16)
            span = pl.ds(top, part.shape[0])
            hi[m, j, span, :] = high
            lo[m, j, span, :] = (part - high.astype(f32)).astype(bf16)
    xg[z] = x_ref[...]
    pl.semaphore_wait(barrier, slots)

    for t in range(1, Z):
        send(xg.at[z], xg.at[z], x_send.at[t], x_recv.at[t], at(0, Z - t))
    send(hi.at[m], other.at[0], w_send.at[0], w_recv.at[0], twin)
    for t in range(1, M):
        send(hi.at[m], hi.at[m], hi_send.at[t], hi_recv.at[t], at(t, 0))

    lane = lax.broadcasted_iota(jnp.int32, (K, 128), 1)
    row = lax.broadcasted_iota(jnp.int32, (K, 128), 0)

    def hidden_part(x, weights, j):
        pre = jnp.dot(x, weights[j, 0:F, :], preferred_element_type=f32)
        pre = pre + weights[j, F + O : rows, :].astype(f32)[0:1]
        hidden = jnp.tanh(pre).astype(bf16)
        return lax.dot_general(
            weights[j, F : F + O, :], hidden, NT, preferred_element_type=f32
        )

    def predict(update, own):
        def step(t, carry):
            if update == 0:
                @pl.when(t > 0)
                def _():
                    settle(xg.at[0], x_recv.at[t])

            target = lax.rem(z - t + Z, Z)
            packed = xg[target].astype(f32)
            x = jnp.concatenate([packed[:, 0:F], packed[:, F:]], axis=0).astype(bf16)
            sums = [hidden_part(x, own, j) for j in range(per)]

            @pl.when(t == 0)
            def _():
                settle(other.at[update], w_recv.at[update])

            here = jnp.where(t == 0, 1.0, 0.0).astype(f32)
            for j in range(per):
                both = sums[j] + hidden_part(x, other.at[update], j)
                both = (both + here * bias[j]).astype(bf16)
                for p in range(M):
                    staged[update, t, p, j * ob : (j + 1) * ob, :] = both[p * ob : (p + 1) * ob, :]

            def post(i, carry):
                to = lax.rem(m + i, M)
                send(
                    staged.at[update, t, to], got.at[update, me],
                    piece_send.at[update], piece_recv.at[update],
                    (to, target * CORES + c),
                )
                return carry

            lax.fori_loop(1, M, post, 0)

            @pl.when(t > 0)
            def _():
                post(0, 0)

            return carry

        lax.fori_loop(0, Z, step, 0)
        got[update, me] = staged[update, 0, m]

    def gain_of(update):
        settle(got.at[update, pl.ds(0, slots - 1)], piece_recv.at[update])
        preds = []
        for p in range(M):
            value = got[update, p].astype(f32)
            for s in range(1, Z):
                value = value + got[update, s * M + p].astype(f32)
            preds += [value[j * ob : (j + 1) * ob] for j in range(per)]
        mean = functools.reduce(jnp.add, preds) * (1.0 / K)
        seen = obs_ref[...]
        for k in range(K):
            span = pl.ds(k * ob, ob)
            anomaly = preds[k] - mean
            misfit = seen + noise_ref[update, span, :].astype(f32) - preds[k]
            for q in range(samples // 128):
                anomalies[q, span, :] = anomaly[:, q * 128 : (q + 1) * 128]
                misfits[q, span, :] = misfit[:, q * 128 : (q + 1) * 128]
        pieces = [(q, o) for q in range(samples // 128) for o in range(ob)]
        a = jnp.concatenate([anomalies[q, pl.ds(o, K, stride=ob), :] for q, o in pieces], axis=1)
        b = jnp.concatenate([misfits[q, pl.ds(o, K, stride=ob), :] for q, o in pieces], axis=1)
        ab = jnp.concatenate([a, b], axis=0)
        ab_high = ab.astype(bf16)
        ab_low = (ab - ab_high.astype(f32)).astype(bf16)
        a_high = a.astype(bf16).astype(f32)
        left = jnp.concatenate([a_high, a - a_high], axis=0).astype(bf16)
        sums = lax.dot_general(left, ab_high, NT, preferred_element_type=f32)
        sums = sums + lax.dot_general(left, ab_low, NT, preferred_element_type=f32)
        pair[update, c] = jnp.zeros((K, 128), f32)
        pair[update, c, :, 0 : 2 * K] = sums[0:K] + sums[K : 2 * K]
        send(pair.at[update, c], pair.at[update, c], pair_send.at[update], pair_recv.at[update], twin)
        settle(pair.at[update, c], pair_recv.at[update])
        every[update, me] = pair[update, 0] + pair[update, 1]

        def post(i, carry):
            send(
                every.at[update, me], every.at[update, me],
                every_send.at[update], every_recv.at[update],
                at(lax.rem(i, M), i // M),
            )
            return carry

        lax.fori_loop(1, slots, post, 0)
        settle(every.at[update, pl.ds(0, slots - 1)], every_recv.at[update])
        system = jnp.sum(every[update], axis=0) * (1.0 / total)
        system = system + jnp.where(lane == row, RIDGE, 0.0)
        for i in range(K):
            pivot = system[i : i + 1, :]
            pivot = pivot / pivot[:, i : i + 1]
            column = system[:, i : i + 1]
            system = jnp.where(row == i, pivot, system - column * pivot)
        return system

    def columns_of(gain):
        return [
            jnp.sum(jnp.where(lane == K + m * per + j, gain, 0.0), axis=1, keepdims=True)
            for j in range(per)
        ]

    def mixed(columns, top, count, base, with_low):
        span = pl.ds(top, count)
        sums = list(base)
        for k in range(K):
            value = hi[k // per, k % per, span, :].astype(f32)
            if with_low:
                value = value + lo[k // per, k % per, span, :].astype(f32)
            for j in range(per):
                sums[j] = sums[j] + columns[j][k : k + 1, :] * value
        return sums

    for j in range(per):
        bias[j] = extra_ref[j].astype(f32)[1:2, 0:O].T

    predict(0, hi.at[m])
    for t in range(1, M):
        send(lo.at[m], lo.at[m], lo_send.at[t], lo_recv.at[t], at(t, 0))
    first = gain_of(0)
    for t in range(1, M):
        settle(hi.at[0], hi_recv.at[t])

    chosen = columns_of(first)
    own_rows = [
        [
            jnp.sum(jnp.where(row[:, 0:1] == m * per + k, chosen[j], 0.0), axis=0, keepdims=True)
            for k in range(per)
        ]
        for j in range(per)
    ]

    def renew(top, count, base):
        sums = mixed(chosen, top, count, base, False)
        for k in range(per):
            rest = lo[m, k, pl.ds(top, count), :].astype(f32)
            for j in range(per):
                sums[j] = sums[j] + own_rows[j][k] * rest
        for j in range(per):
            fresh[j, pl.ds(top, count), :] = sums[j].astype(bf16)
        return sums

    for start, ref, size in ((0, w_in_ref, F), (F, w_out_ref, O)):
        def chunk(i, carry, start=start, ref=ref):
            at_row = pl.multiple_of(i * 16, 16)
            renew(
                pl.multiple_of(start + i * 16, 16), 16,
                [ref[j, pl.ds(at_row, 16), :] for j in range(per)],
            )
            return carry

        lax.fori_loop(0, size // 16, chunk, 0)
    tail = renew(F + O, 16, [extra_ref[j] for j in range(per)])
    for j in range(per):
        bias[j] = tail[j][1:2, 0:O].T
    send(fresh, other.at[1], w_send.at[1], w_recv.at[1], twin)

    predict(1, fresh)
    second = gain_of(1)
    for t in range(1, M):
        settle(lo.at[0], lo_recv.at[t])

    joint = first + second
    for i in range(K):
        joint = joint + first[:, K + i : K + i + 1] * second[i : i + 1, :]
    chosen_both = columns_of(joint)
    for start, ref, out, size in ((0, w_in_ref, new_in_ref, F), (F, w_out_ref, new_out_ref, O)):
        def finish(i, carry, start=start, ref=ref, out=out):
            at_row = pl.multiple_of(i * 16, 16)
            sums = mixed(
                chosen_both, pl.multiple_of(start + i * 16, 16), 16,
                [ref[j, pl.ds(at_row, 16), :] for j in range(per)], True,
            )
            for j in range(per):
                out[j, pl.ds(at_row, 16), :] = sums[j]
            return carry

        lax.fori_loop(0, size // 16, finish, 0)
    sums = mixed(chosen_both, F + O, 16, [extra_ref[j] for j in range(per)], True)
    for j in range(per):
        new_extra_ref[j] = sums[j]

    for t in range(1, Z):
        settle(xg.at[0], x_send.at[t])
    for t in range(1, M):
        settle(hi.at[0], hi_send.at[t])
        settle(lo.at[0], lo_send.at[t])
    for update in range(UPDATES):
        settle(fresh, w_send.at[update])
        settle(got.at[update, pl.ds(0, slots - 1)], piece_send.at[update])
        settle(pair.at[update, 0], pair_send.at[update])
        settle(every.at[update, pl.ds(0, slots - 1)], every_send.at[update])


def on_device(M, Z, inputs, observed, noise, w_in, b_in, w_out, b_out):
    f32, bf16 = jnp.float32, jnp.bfloat16
    per, F, hl = w_in.shape
    O = w_out.shape[1]
    K = per * M
    ob, samples = observed.shape
    half = samples // 2
    rows = F + O + 16
    slots = Z * M
    packed = jnp.concatenate([inputs[:half], inputs[half:]], axis=1)
    extra = jnp.concatenate(
        [b_in[:, None, :], jnp.pad(b_out, ((0, 0), (0, hl - O)))[:, None, :], jnp.zeros((per, 14, hl), f32)],
        axis=1,
    )
    total = float(O * samples * CORES * Z)
    vmem = pl.BlockSpec(memory_space=pltpu.VMEM)
    dma = pltpu.SemaphoreType.DMA
    new_in, new_out, new_extra = pl.pallas_call(
        functools.partial(kernel, M, Z, total),
        out_shape=(
            jax.ShapeDtypeStruct(w_in.shape, f32),
            jax.ShapeDtypeStruct(w_out.shape, f32),
            jax.ShapeDtypeStruct(extra.shape, f32),
        ),
        in_specs=[vmem] * 6,
        out_specs=(vmem,) * 3,
        scratch_shapes=[
            pltpu.VMEM((Z, half, 2 * F), bf16),
            pltpu.VMEM((M, per, rows, hl), bf16),
            pltpu.VMEM((M, per, rows, hl), bf16),
            pltpu.VMEM((per, rows, hl), bf16),
            pltpu.VMEM((UPDATES, per, rows, hl), bf16),
            pltpu.VMEM((per, O, 1), f32),
            pltpu.VMEM((UPDATES, Z, M, per * ob, samples), bf16),
            pltpu.VMEM((UPDATES, slots, per * ob, samples), bf16),
            pltpu.VMEM((samples // 128, K * ob, 128), f32),
            pltpu.VMEM((samples // 128, K * ob, 128), f32),
            pltpu.VMEM((UPDATES, CORES, K, 128), f32),
            pltpu.VMEM((UPDATES, slots, K, 128), f32),
            dma((Z,)), dma((Z,)),
            dma((M,)), dma((M,)),
            dma((M,)), dma((M,)),
            dma((UPDATES,)), dma((UPDATES,)),
            dma((UPDATES,)), dma((UPDATES,)),
            dma((UPDATES,)), dma((UPDATES,)),
            dma((UPDATES,)), dma((UPDATES,)),
        ],
        compiler_params=pltpu.CompilerParams(
            collective_id=0, has_side_effects=True, vmem_limit_bytes=40 * 1024 * 1024
        ),
        name="inversion",
    )(packed, observed, noise.reshape(UPDATES, K * ob, samples), w_in, w_out, extra)
    return new_in, new_extra[:, 0, :], new_out, new_extra[:, 1, :O]


def solution(mesh):
    placed = (
        P("dp", None),
        P("member", "dp"),
        P(None, None, "member", "dp"),
        P("member", None, "dp"),
        P("member", "dp"),
        P("member", None, "dp"),
        P("member", None),
    )
    return jax.shard_map(
        functools.partial(on_device, mesh.shape["member"], mesh.shape["dp"] // CORES),
        mesh=mesh,
        in_specs=placed,
        out_specs=(
            P("member", None, "dp"),
            P("member", "dp"),
            P("member", None, "dp"),
            P("member", None),
        ),
        check_vma=False,
    )
```

time: 257 us -> 66.1 us (0.26)
  blocking collectives: 140 us -> 0 us
  Pallas kernels: 0 us -> 57.5 us
  waiting for transfers between devices: 51.6 us -> 0 us
  matrix products: 24.6 us -> 0 us
  between operations: 14.5 us -> 0.69 us
  other arithmetic: 9.31 us -> 0.16 us
  starting transfers between devices: 7.2 us -> 0 us
    psum x2 -> x0, blocking collectives: 79.9 us -> none  [on_device(): gram, cross = lax.psum((gram_part, cross_part), ('member', 'dp'))]
    all_gather x6 -> x0, blocking collectives: 60.6 us -> none  [the longest x2 27.2 us: predict(): lax.all_gather(shards[2], 'dp', axis=2, tiled=True)]
    pallas_call x0 -> x1, Pallas kernels: none -> 57.5 us  [on_device(): pl.pallas_call(functools.partial(kernel, M, Z, total), out_shape=(jax.Sha...]
    all_gather x8 -> x0, waiting for transfers between devices: 45.7 us -> none  [the longest x2 36.5 us: predict(): lax.all_gather(shards[0], 'dp', axis=2, tiled=True)]
    dot_general x16 -> x0, matrix products: 23.8 us -> none  [the longest x8 14.3 us: mix_own(): lax.dot_general(columns, flat, (((0,), (0,)), ((), ())), precision=lax.Pr...]
    all_to_all x2 -> x0, starting transfers between devices: 6.91 us -> none  [on_device(): lax.all_to_all(predicted.astype(jnp.bfloat16), 'member', split_axis=1, co...]
    another operation x10 -> x0, other arithmetic: 5.33 us -> none  [the longest x6 2.79 us: solve_gain(): factor = jnp.linalg.cholesky(gram + ridge_level * eye)]
    all_to_all x2 -> x0, waiting for transfers between devices: 4.53 us -> none  [on_device(): lax.all_to_all(predicted.astype(jnp.bfloat16), 'member', split_axis=1, co...]
  transfers between devices with their start and end apart: 10 -> 0, of which waited for: 4 -> 0; matrix products, arithmetic and copies ran while one was open for 15% -> 0% of each run, Pallas kernels for 0% -> 0%
where the time goes in v1:
time: 66.1 us; the launch traced here: 65.8 us
  Pallas kernels  57.5 us (87%)
  local copies, waits for them, and re-layouts  7.44 us (11%)
  between operations  0.69 us (1%)
    pallas_call x1, Pallas kernels, on_device(): pl.pallas_call(functools.partial(kernel, M, Z, total), out_shape=(jax.Sha...  57.5 us
    unnamed x17, local copies, waits for them, and re-layouts  6 us

profile of v1, /device:TPU:0, one launch (start us, length us, event | category | flops | bytes accessed | tf_op | source)
XLA Modules:
  0.0 65.8 jit_solution(7134307748498322427)
XLA Ops:
  0.6 0.0 copy-start
  0.6 0.8 %fusion = (bf16[128,64]{0,1:T(8,128)(2,1)S(1)}, bf16[128,64]{0,1:T(8,128)(2,1)S(1)}) fusion(bf16[256,64]{0,1:T(8,128)(2,1)} %param.7), kind=kLoop, calls=%fused_computation.3 | loop fusion | bytes 65536 | tf_op jit(solution)/shard_map/slice | solution.py:290
  1.4 0.1 copy.14
  1.5 0.1 copy.15
  1.7 0.0 copy-start.5
  1.7 0.1 pad_maximum_fusion.x_ref
  1.8 0.6 copy-done.5
  2.4 0.0 copy-start.4
  2.4 0.7 %copy-done.4 = f32[2,512]{1,0:T(2,128)S(1)} copy-done((f32[2,512]{1,0:T(2,128)S(1)}, f32[2,512]{1,0:T(2,128)}, u32[]{:S(2)}) %copy-start.4) | copy-done | bytes 4120
  3.1 0.1 pad.7.clone
  3.1 0.0 copy-start.3
  3.1 0.1 maximum_maximum_fusion.extra_ref
  3.2 0.0 copy-done
  3.2 0.6 copy-done.3
  3.8 0.0 copy-start.1
  3.9 0.9 %copy-done.1 = f32[2,64,512]{2,1,0:T(8,128)S(1)} copy-done((f32[2,64,512]{2,1,0:T(8,128)S(1)}, f32[2,64,512]{2,1,0:T(8,128)}, u32[]{:S(2)}) %copy-start.1) | copy-done | bytes 262168
  4.8 0.0 copy-start.2
  4.8 0.9 %copy-done.2 = bf16[2,8,16,256]{3,2,1,0:T(8,128)(2,1)S(1)} copy-done((bf16[2,8,16,256]{3,2,1,0:T(8,128)(2,1)S(1)}, bf16[2,8,16,256]{3,2,1,0:T(8,128)(2,1)}, u32[]{:S(2)}) %copy-start.2) | copy-done | bytes 131096
  5.7 57.5 %inversion.1 = (f32[2,64,512]{2,1,0:T(8,128)S(1)}, f32[2,64,512]{2,1,0:T(8,128)S(1)}, f32[2,16,512]{2,1,0:T(8,128)S(1)}) custom-call(bf16[128,128]{1,0:T(8,128)(2,1)S(1)} %pad_maximum_fusion.x_ref, f32[16,256]{1,0:T(8,128)S(1)} %copy-done.3, bf16[2,128,256]{2,1,0:T(8,128)(2,1)S(1)} %bitcast.5, f32[2,64,512]{2,1,0:T(8,128)S(1)} %copy-done, ...), custom_call_target="tpu_custom_call" | custom-call | tf_op jit(solution)/shard_map/inversion/pallas_call | solution.py:298
  63.2 0.6 copy.17
  63.8 0.6 slice.15
  64.4 0.7 %copy.20 = f32[2,64,512]{2,1,0:T(8,128)} copy(f32[2,64,512]{2,1,0:T(8,128)S(1)} %get-tuple-element.16) | data formatting | bytes 524288
  65.1 0.7 %copy.21 = f32[2,64,512]{2,1,0:T(8,128)} copy(f32[2,64,512]{2,1,0:T(8,128)S(1)} %get-tuple-element.18) | data formatting | bytes 524288
  (5 shorter events, 0.0 us)
Async XLA Ops:
  0.6 2.6 %copy-start = (f32[2,64,512]{2,1,0:T(8,128)S(1)}, f32[2,64,512]{2,1,0:T(8,128)}, u32[]{:S(2)}) copy-start(f32[2,64,512]{2,1,0:T(8,128)} %w_in_ref.1) | copy-start | bytes 786436
  1.7 0.7 %copy-start.5 = (f32[2,64]{1,0:T(2,128)S(1)}, f32[2,64]{1,0:T(2,128)}, u32[]{:S(2)}) copy-start(f32[2,64]{1,0:T(2,128)} %param.13) | copy-start | bytes 1540
  2.4 0.7 %copy-start.4 = (f32[2,512]{1,0:T(2,128)S(1)}, f32[2,512]{1,0:T(2,128)}, u32[]{:S(2)}) copy-start(f32[2,512]{1,0:T(2,128)} %param.11) | copy-start | bytes 12292
  3.1 0.7 %copy-start.3 = (f32[16,256]{1,0:T(8,128)S(1)}, f32[16,256]{1,0:T(8,128)}, u32[]{:S(2)}) copy-start(f32[16,256]{1,0:T(8,128)} %obs_ref.1) | copy-start | bytes 49156
  3.8 0.9 %copy-start.1 = (f32[2,64,512]{2,1,0:T(8,128)S(1)}, f32[2,64,512]{2,1,0:T(8,128)}, u32[]{:S(2)}) copy-start(f32[2,64,512]{2,1,0:T(8,128)} %w_out_ref.1) | copy-start | bytes 786436
  4.8 0.9 %copy-start.2 = (bf16[2,8,16,256]{3,2,1,0:T(8,128)(2,1)S(1)}, bf16[2,8,16,256]{3,2,1,0:T(8,128)(2,1)}, u32[]{:S(2)}) copy-start(bf16[2,8,16,256]{3,2,1,0:T(8,128)(2,1)} %param.9) | copy-start | bytes 393220

commit v2 on v1

--- a/solution.py
+++ b/solution.py
@@ -16,9 +16,10 @@
 
 def kernel(
     M, Z, total,
-    x_ref, obs_ref, noise_ref, w_in_ref, w_out_ref, extra_ref,
-    new_in_ref, new_out_ref, new_extra_ref,
-    xg, hi, lo, fresh, other, bias, staged, got, anomalies, misfits, pair, every,
+    x_hbm, obs_hbm, noise_hbm, w_in_hbm, b_in_hbm, w_out_hbm, b_out_hbm,
+    new_in_ref, new_b_in_ref, new_out_ref, new_b_out_ref,
+    obs_ref, noise_ref, w_in_ref, b_in_ref, w_out_ref, b_out_ref, extra_ref, load_sem,
+    xg, turned, hi, lo, fresh, other, bias, staged, got, anomalies, misfits, pair, every,
     x_send, x_recv, hi_send, hi_recv, lo_send, lo_recv, w_send, w_recv,
     piece_send, piece_recv, pair_send, pair_recv, every_send, every_recv,
 ):
@@ -32,6 +33,7 @@
     ob = O // M
     samples = noise_ref.shape[2]
     rows = hi.shape[2]
+    A = rows - O
     slots = Z * M
     me = z * M + m
     twin = (m, z * CORES + (1 - c))
@@ -48,6 +50,16 @@
     def settle(ref, sem):
         pltpu.make_async_copy(ref, ref, sem).wait()
 
+    loads = [
+        pltpu.make_async_copy(src, dst, load_sem.at[i])
+        for i, (src, dst) in enumerate((
+            (x_hbm, xg.at[z, pl.ds(0, F)]), (w_in_hbm, w_in_ref), (b_in_hbm, b_in_ref),
+            (b_out_hbm, b_out_ref), (w_out_hbm, w_out_ref), (obs_hbm, obs_ref), (noise_hbm, noise_ref),
+        ))
+    ]
+    for load in loads:
+        load.start()
+
     barrier = pltpu.get_barrier_semaphore()
     pl.semaphore_signal(barrier, inc=1, device_id=twin, device_id_type=MESH)
 
@@ -59,17 +71,28 @@
 
     lax.fori_loop(1, slots, greet, 0)
 
-    for j in range(per):
-        for top, part in ((0, w_in_ref[j]), (F, w_out_ref[j]), (F + O, extra_ref[j])):
+    ones = jnp.where(lax.broadcasted_iota(jnp.int32, (16, samples), 0) == 0, 1.0, 0.0)
+    for i in range(Z):
+        xg[i, F:A, :] = ones.astype(bf16)
+    for load in loads[1:4]:
+        load.wait()
+    extra_ref[...] = jnp.zeros_like(extra_ref)
+    for j in range(per):
+        extra_ref[j, 0:1, :] = b_in_ref[j : j + 1, :]
+        extra_ref[j, 1:2, 0:O] = b_out_ref[j : j + 1, :]
+    loads[4].wait()
+
+    for j in range(per):
+        for top, part in ((0, w_in_ref[j]), (F, extra_ref[j]), (A, w_out_ref[j])):
             high = part.astype(bf16)
             span = pl.ds(top, part.shape[0])
             hi[m, j, span, :] = high
             lo[m, j, span, :] = (part - high.astype(f32)).astype(bf16)
-    xg[z] = x_ref[...]
+    loads[0].wait()
     pl.semaphore_wait(barrier, slots)
 
     for t in range(1, Z):
-        send(xg.at[z], xg.at[z], x_send.at[t], x_recv.at[t], at(0, Z - t))
+        send(xg.at[z, pl.ds(0, F)], xg.at[z, pl.ds(0, F)], x_send.at[t], x_recv.at[t], at(0, Z - t))
     send(hi.at[m], other.at[0], w_send.at[0], w_recv.at[0], twin)
     for t in range(1, M):
         send(hi.at[m], hi.at[m], hi_send.at[t], hi_recv.at[t], at(t, 0))
@@ -77,33 +100,36 @@
     lane = lax.broadcasted_iota(jnp.int32, (K, 128), 1)
     row = lax.broadcasted_iota(jnp.int32, (K, 128), 0)
 
-    def hidden_part(x, weights, j):
-        pre = jnp.dot(x, weights[j, 0:F, :], preferred_element_type=f32)
-        pre = pre + weights[j, F + O : rows, :].astype(f32)[0:1]
+    def turn(half, weights):
+        for j in range(per):
+            turned[half, j] = weights[j, 0:A, :].astype(f32).T.astype(bf16)
+
+    def hidden_part(x, half, weights, j):
+        pre = jnp.dot(turned[half, j], x, preferred_element_type=f32)
         hidden = jnp.tanh(pre).astype(bf16)
-        return lax.dot_general(
-            weights[j, F : F + O, :], hidden, NT, preferred_element_type=f32
-        )
+        return jnp.dot(weights[j, A:rows, :], hidden, preferred_element_type=f32)
 
     def predict(update, own):
+        turn(0, own)
+
         def step(t, carry):
             if update == 0:
                 @pl.when(t > 0)
                 def _():
-                    settle(xg.at[0], x_recv.at[t])
+                    settle(xg.at[0, pl.ds(0, F)], x_recv.at[t])
 
             target = lax.rem(z - t + Z, Z)
-            packed = xg[target].astype(f32)
-            x = jnp.concatenate([packed[:, 0:F], packed[:, F:]], axis=0).astype(bf16)
-            sums = [hidden_part(x, own, j) for j in range(per)]
+            x = xg[target]
+            sums = [hidden_part(x, 0, own, j) for j in range(per)]
 
             @pl.when(t == 0)
             def _():
                 settle(other.at[update], w_recv.at[update])
+                turn(1, other.at[update])
 
             here = jnp.where(t == 0, 1.0, 0.0).astype(f32)
             for j in range(per):
-                both = sums[j] + hidden_part(x, other.at[update], j)
+                both = sums[j] + hidden_part(x, 1, other.at[update], j)
                 both = (both + here * bias[j]).astype(bf16)
                 for p in range(M):
                     staged[update, t, p, j * ob : (j + 1) * ob, :] = both[p * ob : (p + 1) * ob, :]
@@ -136,6 +162,9 @@
             for s in range(1, Z):
                 value = value + got[update, s * M + p].astype(f32)
             preds += [value[j * ob : (j + 1) * ob] for j in range(per)]
+        if update == 0:
+            for load in loads[5:]:
+                load.wait()
         mean = functools.reduce(jnp.add, preds) * (1.0 / K)
         seen = obs_ref[...]
         for k in range(K):
@@ -226,7 +255,7 @@
             fresh[j, pl.ds(top, count), :] = sums[j].astype(bf16)
         return sums
 
-    for start, ref, size in ((0, w_in_ref, F), (F, w_out_ref, O)):
+    for start, ref, size in ((0, w_in_ref, F), (A, w_out_ref, O)):
         def chunk(i, carry, start=start, ref=ref):
             at_row = pl.multiple_of(i * 16, 16)
             renew(
@@ -236,7 +265,7 @@
             return carry
 
         lax.fori_loop(0, size // 16, chunk, 0)
-    tail = renew(F + O, 16, [extra_ref[j] for j in range(per)])
+    tail = renew(F, 16, [extra_ref[j] for j in range(per)])
     for j in range(per):
         bias[j] = tail[j][1:2, 0:O].T
     send(fresh, other.at[1], w_send.at[1], w_recv.at[1], twin)
@@ -250,7 +279,7 @@
     for i in range(K):
         joint = joint + first[:, K + i : K + i + 1] * second[i : i + 1, :]
     chosen_both = columns_of(joint)
-    for start, ref, out, size in ((0, w_in_ref, new_in_ref, F), (F, w_out_ref, new_out_ref, O)):
+    for start, ref, out, size in ((0, w_in_ref, new_in_ref, F), (A, w_out_ref, new_out_ref, O)):
         def finish(i, carry, start=start, ref=ref, out=out):
             at_row = pl.multiple_of(i * 16, 16)
             sums = mixed(
@@ -262,12 +291,13 @@
             return carry
 
         lax.fori_loop(0, size // 16, finish, 0)
-    sums = mixed(chosen_both, F + O, 16, [extra_ref[j] for j in range(per)], True)
-    for j in range(per):
-        new_extra_ref[j] = sums[j]
+    sums = mixed(chosen_both, F, 16, [extra_ref[j] for j in range(per)], True)
+    for j in range(per):
+        new_b_in_ref[j : j + 1, :] = sums[j][0:1]
+        new_b_out_ref[j : j + 1, :] = sums[j][1:2, 0:O]
 
     for t in range(1, Z):
-        settle(xg.at[0], x_send.at[t])
+        settle(xg.at[0, pl.ds(0, F)], x_send.at[t])
     for t in range(1, M):
         settle(hi.at[0], hi_send.at[t])
         settle(lo.at[0], lo_send.at[t])
@@ -284,28 +314,30 @@
     O = w_out.shape[1]
     K = per * M
     ob, samples = observed.shape
-    half = samples // 2
     rows = F + O + 16
     slots = Z * M
-    packed = jnp.concatenate([inputs[:half], inputs[half:]], axis=1)
-    extra = jnp.concatenate(
-        [b_in[:, None, :], jnp.pad(b_out, ((0, 0), (0, hl - O)))[:, None, :], jnp.zeros((per, 14, hl), f32)],
-        axis=1,
-    )
     total = float(O * samples * CORES * Z)
     vmem = pl.BlockSpec(memory_space=pltpu.VMEM)
     dma = pltpu.SemaphoreType.DMA
-    new_in, new_out, new_extra = pl.pallas_call(
+    hbm = pl.BlockSpec(memory_space=pltpu.HBM)
+    return pl.pallas_call(
         functools.partial(kernel, M, Z, total),
-        out_shape=(
-            jax.ShapeDtypeStruct(w_in.shape, f32),
-            jax.ShapeDtypeStruct(w_out.shape, f32),
-            jax.ShapeDtypeStruct(extra.shape, f32),
+        out_shape=tuple(
+            jax.ShapeDtypeStruct(own.shape, f32) for own in (w_in, b_in, w_out, b_out)
         ),
-        in_specs=[vmem] * 6,
-        out_specs=(vmem,) * 3,
+        in_specs=[hbm] * 7,
+        out_specs=(vmem,) * 4,
         scratch_shapes=[
-            pltpu.VMEM((Z, half, 2 * F), bf16),
+            pltpu.VMEM((ob, samples), f32),
+            pltpu.VMEM((UPDATES, K * ob, samples), bf16),
+            pltpu.VMEM(w_in.shape, f32),
+            pltpu.VMEM(b_in.shape, f32),
+            pltpu.VMEM(w_out.shape, f32),
+            pltpu.VMEM(b_out.shape, f32),
+            pltpu.VMEM((per, 16, hl), f32),
+            dma((7,)),
+            pltpu.VMEM((Z, F + 16, samples), bf16),
+            pltpu.VMEM((CORES, per, hl, F + 16), bf16),
             pltpu.VMEM((M, per, rows, hl), bf16),
             pltpu.VMEM((M, per, rows, hl), bf16),
             pltpu.VMEM((per, rows, hl), bf16),
@@ -326,11 +358,10 @@
             dma((UPDATES,)), dma((UPDATES,)),
         ],
         compiler_params=pltpu.CompilerParams(
-            collective_id=0, has_side_effects=True, vmem_limit_bytes=40 * 1024 * 1024
+            collective_id=0, has_side_effects=True, vmem_limit_bytes=56 * 1024 * 1024
         ),
         name="inversion",
-    )(packed, observed, noise.reshape(UPDATES, K * ob, samples), w_in, w_out, extra)
-    return new_in, new_extra[:, 0, :], new_out, new_extra[:, 1, :O]
+    )(inputs.T, observed, noise.reshape(UPDATES, K * ob, samples), w_in, b_in, w_out, b_out)
 
 
 def solution(mesh):

time: 66.1 us -> 63.5 us (0.961)
  local copies, waits for them, and re-layouts: 7.44 us -> 3.58 us
  Pallas kernels: 57.5 us -> 59.1 us
    unnamed x17 -> x10, local copies, waits for them, and re-layouts: 6 us -> 3.58 us
    pallas_call x1, Pallas kernels: 57.5 us -> 59.1 us  [on_device(): pl.pallas_call(functools.partial(kernel, M, Z, total), out_shape=tuple((j...]
    slice x3 -> x0, local copies, waits for them, and re-layouts: 1.35 us -> none  [the longest x1 0.78 us: on_device(): packed = jnp.concatenate([inputs[:half], inputs[half:]], axis=1)]
where the time goes in v2:
time: 63.5 us; the launch traced here: 63.3 us
  Pallas kernels  59.1 us (93%)
  local copies, waits for them, and re-layouts  3.58 us (6%)
  between operations  0.66 us (1%)
    pallas_call x1, Pallas kernels, on_device(): pl.pallas_call(functools.partial(kernel, M, Z, total), out_shape=tuple((j...  59.1 us
    unnamed x10, local copies, waits for them, and re-layouts  3.58 us

profile of v2, /device:TPU:0, one launch (start us, length us, event | category | flops | bytes accessed | tf_op | source)
XLA Modules:
  0.0 63.3 jit_solution(12029210591390228487)
XLA Ops:
  0.6 59.1 %inversion.1 = (f32[2,64,512]{2,1,0:T(8,128)}, f32[2,512]{1,0:T(2,128)}, f32[2,64,512]{2,1,0:T(8,128)}, f32[2,64]{1,0:T(2,128)}) custom-call(bf16[64,256]{1,0:T(8,128)(2,1)} %bitcast.3, f32[16,256]{1,0:T(8,128)} %obs_hbm.1, bf16[2,128,256]{2,1,0:T(8,128)(2,1)} %bitcast.2, f32[2,64,512]{2,1,0:T(8,128)} %w_in_hbm.1, f32[2,512]{1,0:T(2,128)} %b_in_hbm.1, ...), custom_call_target="tpu_custom_call" | custom-call | tf_op jit(solution)/shard_map/inversion/pallas_call | solution.py:323
  59.7 0.0 copy-start.1
  59.7 0.0 copy-start
  59.8 1.7 %copy.15 = f32[2,64,512]{2,1,0:T(8,128)} copy(f32[2,64,512]{2,1,0:T(8,128)} %get-tuple-element.8) | data formatting | bytes 524288
  61.5 0.0 copy-done.1
  61.5 0.6 copy.16
  62.1 0.0 copy-done
  62.1 0.0 copy-start.2
  62.1 0.7 %copy.17 = f32[2,64,512]{2,1,0:T(8,128)} copy(f32[2,64,512]{2,1,0:T(8,128)S(1)} %copy-done) | data formatting | bytes 524288
  62.8 0.0 copy-done.2
  62.8 0.6 copy.18
Async XLA Ops:
  59.7 1.7 %copy-start.1 = (f32[2,512]{1,0:T(2,128)S(1)}, f32[2,512]{1,0:T(2,128)}, u32[]{:S(2)}) copy-start(f32[2,512]{1,0:T(2,128)} %get-tuple-element.9) | copy-start | bytes 12292
  59.7 2.3 %copy-start = (f32[2,64,512]{2,1,0:T(8,128)S(1)}, f32[2,64,512]{2,1,0:T(8,128)}, u32[]{:S(2)}) copy-start(f32[2,64,512]{2,1,0:T(8,128)} %get-tuple-element.10) | copy-start | bytes 786436
  62.1 0.7 %copy-start.2 = (f32[2,64]{1,0:T(2,128)S(1)}, f32[2,64]{1,0:T(2,128)}, u32[]{:S(2)}) copy-start(f32[2,64]{1,0:T(2,128)} %get-tuple-element.11) | copy-start | bytes 1540

commit v3 on v2

--- a/solution.py
+++ b/solution.py
@@ -10,6 +10,8 @@
 UPDATES = 2
 RIDGE = 0.5
 CORES = 2
+IN_SCALE, BIAS_SCALE, OUT_SCALE = 2.0**15, 2.0**13, 2.0**18
+TINY = 2.0**-125
 MESH = pl.DeviceIdType.MESH
 NT = (((1,), (1,)), ((), ()))
 
@@ -19,8 +21,8 @@
     x_hbm, obs_hbm, noise_hbm, w_in_hbm, b_in_hbm, w_out_hbm, b_out_hbm,
     new_in_ref, new_b_in_ref, new_out_ref, new_b_out_ref,
     obs_ref, noise_ref, w_in_ref, b_in_ref, w_out_ref, b_out_ref, extra_ref, load_sem,
-    xg, turned, hi, lo, fresh, other, bias, staged, got, anomalies, misfits, pair, every,
-    x_send, x_recv, hi_send, hi_recv, lo_send, lo_recv, w_send, w_recv,
+    xg, turned, own, code, full, fresh, other, bias, staged, got, anomalies, misfits, pair, every,
+    x_send, x_recv, code_send, code_recv, w_send, w_recv,
     piece_send, piece_recv, pair_send, pair_recv, every_send, every_recv,
 ):
     f32, bf16 = jnp.float32, jnp.bfloat16
@@ -32,7 +34,7 @@
     K = per * M
     ob = O // M
     samples = noise_ref.shape[2]
-    rows = hi.shape[2]
+    rows = own.shape[1]
     A = rows - O
     slots = Z * M
     me = z * M + m
@@ -83,19 +85,24 @@
     loads[4].wait()
 
     for j in range(per):
-        for top, part in ((0, w_in_ref[j]), (F, extra_ref[j]), (A, w_out_ref[j])):
-            high = part.astype(bf16)
+        for top, part, scale in (
+            (0, w_in_ref[j], IN_SCALE), (F, extra_ref[j], BIAS_SCALE), (A, w_out_ref[j], OUT_SCALE)
+        ):
             span = pl.ds(top, part.shape[0])
-            hi[m, j, span, :] = high
-            lo[m, j, span, :] = (part - high.astype(f32)).astype(bf16)
+            own[j, span, :] = part.astype(bf16)
+            full[m, j, span, :] = part
+            power = part * scale
+            for _ in range(3):
+                power = power * power
+            code[m, j, span, :] = jnp.where(part < 0, -power, power).astype(bf16)
     loads[0].wait()
     pl.semaphore_wait(barrier, slots)
 
     for t in range(1, Z):
         send(xg.at[z, pl.ds(0, F)], xg.at[z, pl.ds(0, F)], x_send.at[t], x_recv.at[t], at(0, Z - t))
-    send(hi.at[m], other.at[0], w_send.at[0], w_recv.at[0], twin)
+    send(own, other.at[0], w_send.at[0], w_recv.at[0], twin)
     for t in range(1, M):
-        send(hi.at[m], hi.at[m], hi_send.at[t], hi_recv.at[t], at(t, 0))
+        send(code.at[m], code.at[m], code_send.at[t], code_recv.at[t], at(t, 0))
 
     lane = lax.broadcasted_iota(jnp.int32, (K, 128), 1)
     row = lax.broadcasted_iota(jnp.int32, (K, 128), 0)
@@ -108,6 +115,25 @@
         pre = jnp.dot(turned[half, j], x, preferred_element_type=f32)
         hidden = jnp.tanh(pre).astype(bf16)
         return jnp.dot(weights[j, A:rows, :], hidden, preferred_element_type=f32)
+
+    def decode():
+        for t in range(1, M):
+            settle(code.at[0], code_recv.at[t])
+
+        def chunk(i, carry):
+            slot = lax.rem(m + 1 + i // (per * (rows // 16)), M)
+            j = lax.rem(i // (rows // 16), per)
+            top = lax.rem(i, rows // 16) * 16
+            span = pl.ds(pl.multiple_of(top, 16), 16)
+            value = code[slot, j, span, :].astype(f32)
+            scale = jnp.where(top < F, 1 / IN_SCALE, jnp.where(top < A, 1 / BIAS_SCALE, 1 / OUT_SCALE))
+            size = jnp.abs(value)
+            root = jnp.exp2(jnp.log2(jnp.maximum(size, TINY)) * 0.125) * scale
+            root = jnp.where(size < TINY, 0.0, root)
+            full[slot, j, span, :] = jnp.where(value < 0, -root, root)
+            return carry
+
+        lax.fori_loop(0, (M - 1) * per * (rows // 16), chunk, 0, unroll=2)
 
     def predict(update, own):
         turn(0, own)
@@ -199,6 +225,8 @@
             return carry
 
         lax.fori_loop(1, slots, post, 0)
+        if update == 0:
+            decode()
         settle(every.at[update, pl.ds(0, slots - 1)], every_recv.at[update])
         system = jnp.sum(every[update], axis=0) * (1.0 / total)
         system = system + jnp.where(lane == row, RIDGE, 0.0)
@@ -215,13 +243,11 @@
             for j in range(per)
         ]
 
-    def mixed(columns, top, count, base, with_low):
+    def mixed(columns, top, count):
         span = pl.ds(top, count)
-        sums = list(base)
+        sums = [full[m, j, span, :] for j in range(per)]
         for k in range(K):
-            value = hi[k // per, k % per, span, :].astype(f32)
-            if with_low:
-                value = value + lo[k // per, k % per, span, :].astype(f32)
+            value = full[k // per, k % per, span, :]
             for j in range(per):
                 sums[j] = sums[j] + columns[j][k : k + 1, :] * value
         return sums
@@ -229,69 +255,43 @@
     for j in range(per):
         bias[j] = extra_ref[j].astype(f32)[1:2, 0:O].T
 
-    predict(0, hi.at[m])
-    for t in range(1, M):
-        send(lo.at[m], lo.at[m], lo_send.at[t], lo_recv.at[t], at(t, 0))
+    predict(0, own)
     first = gain_of(0)
-    for t in range(1, M):
-        settle(hi.at[0], hi_recv.at[t])
-
     chosen = columns_of(first)
-    own_rows = [
-        [
-            jnp.sum(jnp.where(row[:, 0:1] == m * per + k, chosen[j], 0.0), axis=0, keepdims=True)
-            for k in range(per)
-        ]
-        for j in range(per)
-    ]
-
-    def renew(top, count, base):
-        sums = mixed(chosen, top, count, base, False)
-        for k in range(per):
-            rest = lo[m, k, pl.ds(top, count), :].astype(f32)
-            for j in range(per):
-                sums[j] = sums[j] + own_rows[j][k] * rest
+
+    def renew(top, count):
+        sums = mixed(chosen, top, count)
         for j in range(per):
             fresh[j, pl.ds(top, count), :] = sums[j].astype(bf16)
         return sums
 
-    for start, ref, size in ((0, w_in_ref, F), (A, w_out_ref, O)):
-        def chunk(i, carry, start=start, ref=ref):
-            at_row = pl.multiple_of(i * 16, 16)
-            renew(
-                pl.multiple_of(start + i * 16, 16), 16,
-                [ref[j, pl.ds(at_row, 16), :] for j in range(per)],
-            )
-            return carry
-
-        lax.fori_loop(0, size // 16, chunk, 0)
-    tail = renew(F, 16, [extra_ref[j] for j in range(per)])
+    def chunk(i, carry):
+        renew(pl.multiple_of(i * 16, 16), 16)
+        return carry
+
+    lax.fori_loop(0, rows // 16, chunk, 0)
+    tail = mixed(chosen, F, 16)
     for j in range(per):
         bias[j] = tail[j][1:2, 0:O].T
     send(fresh, other.at[1], w_send.at[1], w_recv.at[1], twin)
 
     predict(1, fresh)
     second = gain_of(1)
-    for t in range(1, M):
-        settle(lo.at[0], lo_recv.at[t])
 
     joint = first + second
     for i in range(K):
         joint = joint + first[:, K + i : K + i + 1] * second[i : i + 1, :]
     chosen_both = columns_of(joint)
-    for start, ref, out, size in ((0, w_in_ref, new_in_ref, F), (A, w_out_ref, new_out_ref, O)):
-        def finish(i, carry, start=start, ref=ref, out=out):
+    for start, out, size in ((0, new_in_ref, F), (A, new_out_ref, O)):
+        def finish(i, carry, start=start, out=out):
             at_row = pl.multiple_of(i * 16, 16)
-            sums = mixed(
-                chosen_both, pl.multiple_of(start + i * 16, 16), 16,
-                [ref[j, pl.ds(at_row, 16), :] for j in range(per)], True,
-            )
+            sums = mixed(chosen_both, pl.multiple_of(start + i * 16, 16), 16)
             for j in range(per):
                 out[j, pl.ds(at_row, 16), :] = sums[j]
             return carry
 
         lax.fori_loop(0, size // 16, finish, 0)
-    sums = mixed(chosen_both, F, 16, [extra_ref[j] for j in range(per)], True)
+    sums = mixed(chosen_both, F, 16)
     for j in range(per):
         new_b_in_ref[j : j + 1, :] = sums[j][0:1]
         new_b_out_ref[j : j + 1, :] = sums[j][1:2, 0:O]
@@ -299,13 +299,21 @@
     for t in range(1, Z):
         settle(xg.at[0, pl.ds(0, F)], x_send.at[t])
     for t in range(1, M):
-        settle(hi.at[0], hi_send.at[t])
-        settle(lo.at[0], lo_send.at[t])
+        settle(code.at[0], code_send.at[t])
     for update in range(UPDATES):
         settle(fresh, w_send.at[update])
         settle(got.at[update, pl.ds(0, slots - 1)], piece_send.at[update])
         settle(pair.at[update, 0], pair_send.at[update])
         settle(every.at[update, pl.ds(0, slots - 1)], every_send.at[update])
+
+
+def place(*refs):
+    sems = refs[8]
+    moves = [pltpu.make_async_copy(refs[i], refs[4 + i], sems.at[i]) for i in range(4)]
+    for move in moves:
+        move.start()
+    for move in moves:
+        move.wait()
 
 
 def on_device(M, Z, inputs, observed, noise, w_in, b_in, w_out, b_out):
@@ -320,7 +328,7 @@
     vmem = pl.BlockSpec(memory_space=pltpu.VMEM)
     dma = pltpu.SemaphoreType.DMA
     hbm = pl.BlockSpec(memory_space=pltpu.HBM)
-    return pl.pallas_call(
+    results = pl.pallas_call(
         functools.partial(kernel, M, Z, total),
         out_shape=tuple(
             jax.ShapeDtypeStruct(own.shape, f32) for own in (w_in, b_in, w_out, b_out)
@@ -338,8 +346,9 @@
             dma((7,)),
             pltpu.VMEM((Z, F + 16, samples), bf16),
             pltpu.VMEM((CORES, per, hl, F + 16), bf16),
+            pltpu.VMEM((per, rows, hl), bf16),
             pltpu.VMEM((M, per, rows, hl), bf16),
-            pltpu.VMEM((M, per, rows, hl), bf16),
+            pltpu.VMEM((M, per, rows, hl), f32),
             pltpu.VMEM((per, rows, hl), bf16),
             pltpu.VMEM((UPDATES, per, rows, hl), bf16),
             pltpu.VMEM((per, O, 1), f32),
@@ -351,7 +360,6 @@
             pltpu.VMEM((UPDATES, slots, K, 128), f32),
             dma((Z,)), dma((Z,)),
             dma((M,)), dma((M,)),
-            dma((M,)), dma((M,)),
             dma((UPDATES,)), dma((UPDATES,)),
             dma((UPDATES,)), dma((UPDATES,)),
             dma((UPDATES,)), dma((UPDATES,)),
@@ -362,6 +370,15 @@
         ),
         name="inversion",
     )(inputs.T, observed, noise.reshape(UPDATES, K * ob, samples), w_in, b_in, w_out, b_out)
+    return pl.pallas_call(
+        place,
+        out_shape=tuple(jax.ShapeDtypeStruct(own.shape, f32) for own in results),
+        in_specs=[hbm] * 4,
+        out_specs=(hbm,) * 4,
+        scratch_shapes=[dma((4,))],
+        compiler_params=pltpu.CompilerParams(vmem_limit_bytes=56 * 1024 * 1024),
+        name="place",
+    )(*results)
 
 
 def solution(mesh):

time: 63.5 us -> 68.1 us (1.072)
  Pallas kernels: 59.1 us -> 67.4 us
  local copies, waits for them, and re-layouts: 3.58 us -> 0 us
    pallas_call x0 -> x1, Pallas kernels: none -> 17.2 us  [on_device(): pl.pallas_call(place, out_shape=tuple((jax.ShapeDtypeStruct(own.shape, f3...]
    pallas_call x1, Pallas kernels: 59.1 us -> 50.2 us  [on_device(): pl.pallas_call(functools.partial(kernel, M, Z, total), out_shape=tuple((j...]
    unnamed x10 -> x0, local copies, waits for them, and re-layouts: 3.58 us -> none
where the time goes in v3:
time: 68.1 us; the launch traced here: 68 us
  Pallas kernels  67.4 us (99%)
    pallas_call x1, Pallas kernels, on_device(): pl.pallas_call(functools.partial(kernel, M, Z, total), out_shape=tuple((j...  50.2 us
    pallas_call x1, Pallas kernels, on_device(): pl.pallas_call(place, out_shape=tuple((jax.ShapeDtypeStruct(own.shape, f3...  17.2 us

profile of v3, /device:TPU:0, one launch (start us, length us, event | category | flops | bytes accessed | tf_op | source)
XLA Modules:
  0.0 68.0 jit_solution(10050455178386206301)
XLA Ops:
  0.6 50.2 %inversion.1 = (f32[2,64,512]{2,1,0:T(8,128)}, f32[2,512]{1,0:T(2,128)}, f32[2,64,512]{2,1,0:T(8,128)}, f32[2,64]{1,0:T(2,128)}) custom-call(bf16[64,256]{1,0:T(8,128)(2,1)} %bitcast.3, f32[16,256]{1,0:T(8,128)} %obs_hbm.1, bf16[2,128,256]{2,1,0:T(8,128)(2,1)} %bitcast.2, f32[2,64,512]{2,1,0:T(8,128)} %w_in_hbm.1, f32[2,512]{1,0:T(2,128)} %b_in_hbm.1, ...), custom_call_target="tpu_custom_call" | custom-call | tf_op jit(solution)/shard_map/inversion/pallas_call | solution.py:331
  50.8 17.2 %place.1 = (f32[2,64,512]{2,1,0:T(8,128)}, f32[2,512]{1,0:T(2,128)}, f32[2,64,512]{2,1,0:T(8,128)}, f32[2,64]{1,0:T(2,128)}) custom-call(f32[2,64,512]{2,1,0:T(8,128)} %get-tuple-element.8.refs_0_, f32[2,512]{1,0:T(2,128)} %get-tuple-element.9.refs_1_, f32[2,64,512]{2,1,0:T(8,128)} %get-tuple-element.10.refs_2_, f32[2,64]{1,0:T(2,128)} %get-tuple-element.11.refs_3_), custom_call_target="tpu_custom_call" | custom-call | tf_op jit(solution)/shard_map/place/pallas_call | solution.py:373

commit v4 on v3

--- a/solution.py
+++ b/solution.py
@@ -40,8 +40,12 @@
     me = z * M + m
     twin = (m, z * CORES + (1 - c))
 
-    def at(dm, dz):
-        return lax.rem(m + dm, M), lax.rem(z - dz + Z, Z) * CORES + c
+    members = [lax.rem(m + i, M) for i in range(M)]
+    places = [lax.rem(z - i + Z, Z) * CORES + c for i in range(Z)]
+
+    pairs = M // 2
+    p_at = [lax.rem(m // 2 + i, pairs) * 2 for i in range(pairs)]
+    q = lax.rem(m, 2)
 
     def send(src, dst, send_sem, recv_sem, target):
         pltpu.make_async_remote_copy(
@@ -65,13 +69,9 @@
     barrier = pltpu.get_barrier_semaphore()
     pl.semaphore_signal(barrier, inc=1, device_id=twin, device_id_type=MESH)
 
-    def greet(i, carry):
-        pl.semaphore_signal(
-            barrier, inc=1, device_id=at(lax.rem(i, M), i // M), device_id_type=MESH
-        )
-        return carry
-
-    lax.fori_loop(1, slots, greet, 0)
+    others = [(members[i % M], places[i // M]) for i in range(1, slots)]
+    for peer in others:
+        pl.semaphore_signal(barrier, inc=1, device_id=peer, device_id_type=MESH)
 
     ones = jnp.where(lax.broadcasted_iota(jnp.int32, (16, samples), 0) == 0, 1.0, 0.0)
     for i in range(Z):
@@ -99,10 +99,14 @@
     pl.semaphore_wait(barrier, slots)
 
     for t in range(1, Z):
-        send(xg.at[z, pl.ds(0, F)], xg.at[z, pl.ds(0, F)], x_send.at[t], x_recv.at[t], at(0, Z - t))
+        send(xg.at[z, pl.ds(0, F)], xg.at[z, pl.ds(0, F)], x_send.at[t], x_recv.at[t], (m, places[Z - t]))
     send(own, other.at[0], w_send.at[0], w_recv.at[0], twin)
-    for t in range(1, M):
-        send(code.at[m], code.at[m], code_send.at[t], code_recv.at[t], at(t, 0))
+    def pass_on(src, sem, target):
+        send(src, src, code_send.at[sem], code_recv.at[sem], (target, places[0]))
+
+    pass_on(code.at[m], 0, p_at[0] + 1 - q)
+    for t in range(1, pairs):
+        pass_on(code.at[m], t, p_at[t] + q)
 
     lane = lax.broadcasted_iota(jnp.int32, (K, 128), 1)
     row = lax.broadcasted_iota(jnp.int32, (K, 128), 0)
@@ -116,9 +120,21 @@
         hidden = jnp.tanh(pre).astype(bf16)
         return jnp.dot(weights[j, A:rows, :], hidden, preferred_element_type=f32)
 
+    cut = per // 2
+    first_half, second_half = pl.ds(0, cut), pl.ds(cut, per - cut)
+
+    def forward():
+        for t in range(pairs):
+            settle(code.at[0], code_recv.at[t])
+        for t in range(1, pairs):
+            pass_on(code.at[p_at[0] + 1 - q, first_half], pairs + t, p_at[t] + q)
+        for t in range(1, pairs):
+            pass_on(code.at[p_at[t] + q, second_half], 2 * pairs + t, p_at[0] + 1 - q)
+
     def decode():
-        for t in range(1, M):
-            settle(code.at[0], code_recv.at[t])
+        for t in range(1, pairs):
+            settle(code.at[0, first_half], code_recv.at[pairs + t])
+            settle(code.at[0, second_half], code_recv.at[2 * pairs + t])
 
         def chunk(i, carry):
             slot = lax.rem(m + 1 + i // (per * (rows // 16)), M)
@@ -138,7 +154,8 @@
     def predict(update, own):
         turn(0, own)
 
-        def step(t, carry):
+        def step(turn_number, carry):
+            t = turn_number if update == 0 else lax.rem(turn_number + 1, Z)
             if update == 0:
                 @pl.when(t > 0)
                 def _():
@@ -148,7 +165,7 @@
             x = xg[target]
             sums = [hidden_part(x, 0, own, j) for j in range(per)]
 
-            @pl.when(t == 0)
+            @pl.when(turn_number == 0)
             def _():
                 settle(other.at[update], w_recv.at[update])
                 turn(1, other.at[update])
@@ -160,20 +177,19 @@
                 for p in range(M):
                     staged[update, t, p, j * ob : (j + 1) * ob, :] = both[p * ob : (p + 1) * ob, :]
 
-            def post(i, carry):
-                to = lax.rem(m + i, M)
+            def post(to):
                 send(
                     staged.at[update, t, to], got.at[update, me],
                     piece_send.at[update], piece_recv.at[update],
                     (to, target * CORES + c),
                 )
-                return carry
-
-            lax.fori_loop(1, M, post, 0)
+
+            for to in members[1:]:
+                post(to)
 
             @pl.when(t > 0)
             def _():
-                post(0, 0)
+                post(m)
 
             return carry
 
@@ -216,15 +232,11 @@
         settle(pair.at[update, c], pair_recv.at[update])
         every[update, me] = pair[update, 0] + pair[update, 1]
 
-        def post(i, carry):
+        for peer in others:
             send(
                 every.at[update, me], every.at[update, me],
-                every_send.at[update], every_recv.at[update],
-                at(lax.rem(i, M), i // M),
+                every_send.at[update], every_recv.at[update], peer,
             )
-            return carry
-
-        lax.fori_loop(1, slots, post, 0)
         if update == 0:
             decode()
         settle(every.at[update, pl.ds(0, slots - 1)], every_recv.at[update])
@@ -256,6 +268,7 @@
         bias[j] = extra_ref[j].astype(f32)[1:2, 0:O].T
 
     predict(0, own)
+    forward()
     first = gain_of(0)
     chosen = columns_of(first)
 
@@ -298,8 +311,11 @@
 
     for t in range(1, Z):
         settle(xg.at[0, pl.ds(0, F)], x_send.at[t])
-    for t in range(1, M):
+    for t in range(pairs):
         settle(code.at[0], code_send.at[t])
+    for t in range(1, pairs):
+        settle(code.at[0, first_half], code_send.at[pairs + t])
+        settle(code.at[0, second_half], code_send.at[2 * pairs + t])
     for update in range(UPDATES):
         settle(fresh, w_send.at[update])
         settle(got.at[update, pl.ds(0, slots - 1)], piece_send.at[update])
@@ -308,12 +324,16 @@
 
 
 def place(*refs):
-    sems = refs[8]
-    moves = [pltpu.make_async_copy(refs[i], refs[4 + i], sems.at[i]) for i in range(4)]
-    for move in moves:
-        move.start()
-    for move in moves:
-        move.wait()
+    held, sems = refs[8:12], refs[12]
+    loads = [pltpu.make_async_copy(refs[i], held[i], sems.at[i]) for i in range(4)]
+    stores = [pltpu.make_async_copy(held[i], refs[4 + i], sems.at[4 + i]) for i in range(4)]
+    for load in loads:
+        load.start()
+    for load, store in zip(loads, stores):
+        load.wait()
+        store.start()
+    for store in stores:
+        store.wait()
 
 
 def on_device(M, Z, inputs, observed, noise, w_in, b_in, w_out, b_out):
@@ -359,7 +379,7 @@
             pltpu.VMEM((UPDATES, CORES, K, 128), f32),
             pltpu.VMEM((UPDATES, slots, K, 128), f32),
             dma((Z,)), dma((Z,)),
-            dma((M,)), dma((M,)),
+            dma((2 * M,)), dma((2 * M,)),
             dma((UPDATES,)), dma((UPDATES,)),
             dma((UPDATES,)), dma((UPDATES,)),
             dma((UPDATES,)), dma((UPDATES,)),
@@ -375,7 +395,7 @@
         out_shape=tuple(jax.ShapeDtypeStruct(own.shape, f32) for own in results),
         in_specs=[hbm] * 4,
         out_specs=(hbm,) * 4,
-        scratch_shapes=[dma((4,))],
+        scratch_shapes=[pltpu.VMEM(own.shape, f32) for own in results] + [dma((8,))],
         compiler_params=pltpu.CompilerParams(vmem_limit_bytes=56 * 1024 * 1024),
         name="place",
     )(*results)

time: 68.1 us -> 47.3 us (0.69)
  Pallas kernels: 67.4 us -> 46.5 us
    pallas_call x1, Pallas kernels: 17.2 us -> 1.82 us  [on_device(): pl.pallas_call(place, out_shape=tuple((jax.ShapeDtypeStruct(own.shape, f3...]
    pallas_call x1, Pallas kernels: 50.2 us -> 44.7 us  [on_device(): pl.pallas_call(functools.partial(kernel, M, Z, total), out_shape=tuple((j...]
where the time goes in v4:
time: 47.3 us; the launch traced here: 47.2 us
  Pallas kernels  46.5 us (98%)
  between operations  0.64 us (1%)
    pallas_call x1, Pallas kernels, on_device(): pl.pallas_call(functools.partial(kernel, M, Z, total), out_shape=tuple((j...  44.7 us
    pallas_call x1, Pallas kernels, on_device(): pl.pallas_call(place, out_shape=tuple((jax.ShapeDtypeStruct(own.shape, f3...  1.82 us

profile of v4, /device:TPU:0, one launch (start us, length us, event | category | flops | bytes accessed | tf_op | source)
XLA Modules:
  0.0 47.2 jit_solution(13537943645959388370)
XLA Ops:
  0.6 44.7 %inversion.1 = (f32[2,64,512]{2,1,0:T(8,128)}, f32[2,512]{1,0:T(2,128)}, f32[2,64,512]{2,1,0:T(8,128)}, f32[2,64]{1,0:T(2,128)}) custom-call(bf16[64,256]{1,0:T(8,128)(2,1)} %bitcast.3, f32[16,256]{1,0:T(8,128)} %obs_hbm.1, bf16[2,128,256]{2,1,0:T(8,128)(2,1)} %bitcast.2, f32[2,64,512]{2,1,0:T(8,128)} %w_in_hbm.1, f32[2,512]{1,0:T(2,128)} %b_in_hbm.1, ...), custom_call_target="tpu_custom_call" | custom-call | tf_op jit(solution)/shard_map/inversion/pallas_call | solution.py:351
  45.4 1.8 %place.1 = (f32[2,64,512]{2,1,0:T(8,128)}, f32[2,512]{1,0:T(2,128)}, f32[2,64,512]{2,1,0:T(8,128)}, f32[2,64]{1,0:T(2,128)}) custom-call(f32[2,64,512]{2,1,0:T(8,128)} %get-tuple-element.8.refs_0_, f32[2,512]{1,0:T(2,128)} %get-tuple-element.9.refs_1_, f32[2,64,512]{2,1,0:T(8,128)} %get-tuple-element.10.refs_2_, f32[2,64]{1,0:T(2,128)} %get-tuple-element.11.refs_3_), custom_call_target="tpu_custom_call" | custom-call | tf_op jit(solution)/shard_map/place/pallas_call | solution.py:393

commit v5 on v4

--- a/solution.py
+++ b/solution.py
@@ -21,9 +21,9 @@
     x_hbm, obs_hbm, noise_hbm, w_in_hbm, b_in_hbm, w_out_hbm, b_out_hbm,
     new_in_ref, new_b_in_ref, new_out_ref, new_b_out_ref,
     obs_ref, noise_ref, w_in_ref, b_in_ref, w_out_ref, b_out_ref, extra_ref, load_sem,
-    xg, turned, own, code, full, fresh, other, bias, staged, got, anomalies, misfits, pair, every,
+    xg, turned, own, code, full, fresh, other, bias, staged, got, anomalies, misfits, wide, every,
     x_send, x_recv, code_send, code_recv, w_send, w_recv,
-    piece_send, piece_recv, pair_send, pair_recv, every_send, every_recv,
+    piece_send, piece_recv, every_send, every_recv,
 ):
     f32, bf16 = jnp.float32, jnp.bfloat16
     m = lax.axis_index("member")
@@ -38,6 +38,9 @@
     A = rows - O
     slots = Z * M
     me = z * M + m
+    devices = slots * CORES
+    mine = d * M + m
+    group = 128 // (2 * K)
     twin = (m, z * CORES + (1 - c))
 
     members = [lax.rem(m + i, M) for i in range(M)]
@@ -67,11 +70,26 @@
         load.start()
 
     barrier = pltpu.get_barrier_semaphore()
-    pl.semaphore_signal(barrier, inc=1, device_id=twin, device_id_type=MESH)
-
-    others = [(members[i % M], places[i // M]) for i in range(1, slots)]
-    for peer in others:
+
+    def greet(peer):
         pl.semaphore_signal(barrier, inc=1, device_id=peer, device_id_type=MESH)
+
+    def everyone(act):
+        for i in range(M):
+            for core in range(CORES):
+                if i or core:
+                    act((members[i], z * CORES + lax.rem(c + core, CORES)))
+
+        def line(dz, carry):
+            place = lax.rem(z + dz, Z) * CORES
+            for i in range(M):
+                for core in range(CORES):
+                    act((members[i], place + core))
+            return carry
+
+        lax.fori_loop(1, Z, line, 0, unroll=Z <= 4)
+
+    everyone(greet)
 
     ones = jnp.where(lax.broadcasted_iota(jnp.int32, (16, samples), 0) == 0, 1.0, 0.0)
     for i in range(Z):
@@ -96,7 +114,7 @@
                 power = power * power
             code[m, j, span, :] = jnp.where(part < 0, -power, power).astype(bf16)
     loads[0].wait()
-    pl.semaphore_wait(barrier, slots)
+    pl.semaphore_wait(barrier, devices - 1)
 
     for t in range(1, Z):
         send(xg.at[z, pl.ds(0, F)], xg.at[z, pl.ds(0, F)], x_send.at[t], x_recv.at[t], (m, places[Z - t]))
@@ -117,7 +135,7 @@
 
     def hidden_part(x, half, weights, j):
         pre = jnp.dot(turned[half, j], x, preferred_element_type=f32)
-        hidden = jnp.tanh(pre).astype(bf16)
+        hidden = jnp.tanh(pre.astype(bf16))
         return jnp.dot(weights[j, A:rows, :], hidden, preferred_element_type=f32)
 
     cut = per // 2
@@ -195,6 +213,13 @@
 
         lax.fori_loop(0, Z, step, 0)
         got[update, me] = staged[update, 0, m]
+
+    def turn_rows(value, way):
+        result = value
+        for g in range(1, group):
+            moved = pltpu.roll(value, (way * g * 2 * K) % 128, 1)
+            result = jnp.where(lax.rem(row, group) == g, moved, result)
+        return result
 
     def gain_of(update):
         settle(got.at[update, pl.ds(0, slots - 1)], piece_recv.at[update])
@@ -226,21 +251,25 @@
         left = jnp.concatenate([a_high, a - a_high], axis=0).astype(bf16)
         sums = lax.dot_general(left, ab_high, NT, preferred_element_type=f32)
         sums = sums + lax.dot_general(left, ab_low, NT, preferred_element_type=f32)
-        pair[update, c] = jnp.zeros((K, 128), f32)
-        pair[update, c, :, 0 : 2 * K] = sums[0:K] + sums[K : 2 * K]
-        send(pair.at[update, c], pair.at[update, c], pair_send.at[update], pair_recv.at[update], twin)
-        settle(pair.at[update, c], pair_recv.at[update])
-        every[update, me] = pair[update, 0] + pair[update, 1]
-
-        for peer in others:
-            send(
-                every.at[update, me], every.at[update, me],
-                every_send.at[update], every_recv.at[update], peer,
+        wide[...] = jnp.zeros((K, 128), f32)
+        wide[:, 0 : 2 * K] = sums[0:K] + sums[K : 2 * K]
+        spread = turn_rows(wide[...], 1)
+        for i in range(K // group):
+            every[update, mine, i : i + 1, :] = jnp.sum(
+                spread[i * group : (i + 1) * group], axis=0, keepdims=True
             )
+        everyone(lambda peer: send(
+            every.at[update, mine], every.at[update, mine],
+            every_send.at[update], every_recv.at[update], peer,
+        ))
         if update == 0:
             decode()
-        settle(every.at[update, pl.ds(0, slots - 1)], every_recv.at[update])
-        system = jnp.sum(every[update], axis=0) * (1.0 / total)
+        settle(every.at[update, pl.ds(0, devices - 1)], every_recv.at[update])
+        lines = jnp.sum(every[update], axis=0) * (1.0 / total)
+        system = jnp.concatenate(
+            [jnp.broadcast_to(lines[i : i + 1], (group, 128)) for i in range(K // group)], axis=0
+        )
+        system = turn_rows(system, -1)
         system = system + jnp.where(lane == row, RIDGE, 0.0)
         for i in range(K):
             pivot = system[i : i + 1, :]
@@ -319,8 +348,7 @@
     for update in range(UPDATES):
         settle(fresh, w_send.at[update])
         settle(got.at[update, pl.ds(0, slots - 1)], piece_send.at[update])
-        settle(pair.at[update, 0], pair_send.at[update])
-        settle(every.at[update, pl.ds(0, slots - 1)], every_send.at[update])
+        settle(every.at[update, pl.ds(0, devices - 1)], every_send.at[update])
 
 
 def place(*refs):
@@ -376,11 +404,10 @@
             pltpu.VMEM((UPDATES, slots, per * ob, samples), bf16),
             pltpu.VMEM((samples // 128, K * ob, 128), f32),
             pltpu.VMEM((samples // 128, K * ob, 128), f32),
-            pltpu.VMEM((UPDATES, CORES, K, 128), f32),
-            pltpu.VMEM((UPDATES, slots, K, 128), f32),
+            pltpu.VMEM((K, 128), f32),
+            pltpu.VMEM((UPDATES, slots * CORES, K * 2 * K // 128, 128), f32),
             dma((Z,)), dma((Z,)),
             dma((2 * M,)), dma((2 * M,)),
-            dma((UPDATES,)), dma((UPDATES,)),
             dma((UPDATES,)), dma((UPDATES,)),
             dma((UPDATES,)), dma((UPDATES,)),
             dma((UPDATES,)), dma((UPDATES,)),

time: 47.3 us -> 45.4 us (0.960)
  Pallas kernels: 46.5 us -> 44.6 us
    pallas_call x1, Pallas kernels: 44.7 us -> 42.8 us  [on_device(): pl.pallas_call(functools.partial(kernel, M, Z, total), out_shape=tuple((j...]
where the time goes in v5:
time: 45.4 us; the launch traced here: 45.2 us
  Pallas kernels  44.6 us (98%)
  between operations  0.64 us (1%)
    pallas_call x1, Pallas kernels, on_device(): pl.pallas_call(functools.partial(kernel, M, Z, total), out_shape=tuple((j...  42.8 us
    pallas_call x1, Pallas kernels, on_device(): pl.pallas_call(place, out_shape=tuple((jax.ShapeDtypeStruct(own.shape, f3...  1.82 us

profile of v5, /device:TPU:0, one launch (start us, length us, event | category | flops | bytes accessed | tf_op | source)
XLA Modules:
  0.0 45.2 jit_solution(17615650942821517604)
XLA Ops:
  0.6 42.8 %inversion.1 = (f32[2,64,512]{2,1,0:T(8,128)}, f32[2,512]{1,0:T(2,128)}, f32[2,64,512]{2,1,0:T(8,128)}, f32[2,64]{1,0:T(2,128)}) custom-call(bf16[64,256]{1,0:T(8,128)(2,1)} %bitcast.3, f32[16,256]{1,0:T(8,128)} %obs_hbm.1, bf16[2,128,256]{2,1,0:T(8,128)(2,1)} %bitcast.2, f32[2,64,512]{2,1,0:T(8,128)} %w_in_hbm.1, f32[2,512]{1,0:T(2,128)} %b_in_hbm.1, ...), custom_call_target="tpu_custom_call" | custom-call | tf_op jit(solution)/shard_map/inversion/pallas_call | solution.py:379
  43.4 1.8 %place.1 = (f32[2,64,512]{2,1,0:T(8,128)}, f32[2,512]{1,0:T(2,128)}, f32[2,64,512]{2,1,0:T(8,128)}, f32[2,64]{1,0:T(2,128)}) custom-call(f32[2,64,512]{2,1,0:T(8,128)} %get-tuple-element.8.refs_0_, f32[2,512]{1,0:T(2,128)} %get-tuple-element.9.refs_1_, f32[2,64,512]{2,1,0:T(8,128)} %get-tuple-element.10.refs_2_, f32[2,64]{1,0:T(2,128)} %get-tuple-element.11.refs_3_), custom_call_target="tpu_custom_call" | custom-call | tf_op jit(solution)/shard_map/place/pallas_call | solution.py:420

commit v6 on v5

--- a/solution.py
+++ b/solution.py
@@ -19,7 +19,7 @@
 def kernel(
     M, Z, total,
     x_hbm, obs_hbm, noise_hbm, w_in_hbm, b_in_hbm, w_out_hbm, b_out_hbm,
-    new_in_ref, new_b_in_ref, new_out_ref, new_b_out_ref,
+    new_in_hbm, new_b_in_hbm, new_out_hbm, new_b_out_hbm,
     obs_ref, noise_ref, w_in_ref, b_in_ref, w_out_ref, b_out_ref, extra_ref, load_sem,
     xg, turned, own, code, full, fresh, other, bias, staged, got, anomalies, misfits, wide, every,
     x_send, x_recv, code_send, code_recv, w_send, w_recv,
@@ -172,19 +172,17 @@
     def predict(update, own):
         turn(0, own)
 
-        def step(turn_number, carry):
+        def step(turn_number):
             t = turn_number if update == 0 else lax.rem(turn_number + 1, Z)
-            if update == 0:
-                @pl.when(t > 0)
-                def _():
-                    settle(xg.at[0, pl.ds(0, F)], x_recv.at[t])
+            peeled = isinstance(turn_number, int)
+            if update == 0 and not peeled:
+                settle(xg.at[0, pl.ds(0, F)], x_recv.at[t])
 
             target = lax.rem(z - t + Z, Z)
             x = xg[target]
             sums = [hidden_part(x, 0, own, j) for j in range(per)]
 
-            @pl.when(turn_number == 0)
-            def _():
+            if peeled:
                 settle(other.at[update], w_recv.at[update])
                 turn(1, other.at[update])
 
@@ -209,9 +207,12 @@
             def _():
                 post(m)
 
+        def block(i, carry):
+            step(i)
             return carry
 
-        lax.fori_loop(0, Z, step, 0)
+        step(0)
+        lax.fori_loop(1, Z, block, 0)
         got[update, me] = staged[update, 0, m]
 
     def turn_rows(value, way):
@@ -324,7 +325,18 @@
     for i in range(K):
         joint = joint + first[:, K + i : K + i + 1] * second[i : i + 1, :]
     chosen_both = columns_of(joint)
-    for start, out, size in ((0, new_in_ref, F), (A, new_out_ref, O)):
+    exits = [
+        pltpu.make_async_copy(src, dst, load_sem.at[n])
+        for n, (src, dst) in enumerate((
+            (w_in_ref, new_in_hbm), (w_out_ref, new_out_hbm),
+            (b_in_ref, new_b_in_hbm), (b_out_ref, new_b_out_hbm),
+        ))
+    ]
+
+    def leave(ref):
+        exits[0 if ref is w_in_ref else 1].start()
+
+    for start, out, size in ((0, w_in_ref, F), (A, w_out_ref, O)):
         def finish(i, carry, start=start, out=out):
             at_row = pl.multiple_of(i * 16, 16)
             sums = mixed(chosen_both, pl.multiple_of(start + i * 16, 16), 16)
@@ -333,11 +345,16 @@
             return carry
 
         lax.fori_loop(0, size // 16, finish, 0)
+        leave(out)
     sums = mixed(chosen_both, F, 16)
     for j in range(per):
-        new_b_in_ref[j : j + 1, :] = sums[j][0:1]
-        new_b_out_ref[j : j + 1, :] = sums[j][1:2, 0:O]
-
+        b_in_ref[j : j + 1, :] = sums[j][0:1]
+        b_out_ref[j : j + 1, :] = sums[j][1:2, 0:O]
+    exits[2].start()
+    exits[3].start()
+
+    for leaving in exits:
+        leaving.wait()
     for t in range(1, Z):
         settle(xg.at[0, pl.ds(0, F)], x_send.at[t])
     for t in range(pairs):
@@ -373,7 +390,6 @@
     rows = F + O + 16
     slots = Z * M
     total = float(O * samples * CORES * Z)
-    vmem = pl.BlockSpec(memory_space=pltpu.VMEM)
     dma = pltpu.SemaphoreType.DMA
     hbm = pl.BlockSpec(memory_space=pltpu.HBM)
     results = pl.pallas_call(
@@ -382,7 +398,7 @@
             jax.ShapeDtypeStruct(own.shape, f32) for own in (w_in, b_in, w_out, b_out)
         ),
         in_specs=[hbm] * 7,
-        out_specs=(vmem,) * 4,
+        out_specs=(hbm,) * 4,
         scratch_shapes=[
             pltpu.VMEM((ob, samples), f32),
             pltpu.VMEM((UPDATES, K * ob, samples), bf16),

time: 45.4 us -> 45 us (level)
  no operation moved by 1% of the time
where the time goes in v6:
time: 45 us; the launch traced here: 44.8 us
  Pallas kernels  44.2 us (98%)
  between operations  0.64 us (1%)
    pallas_call x1, Pallas kernels, on_device(): pl.pallas_call(functools.partial(kernel, M, Z, total), out_shape=tuple((j...  42.4 us
    pallas_call x1, Pallas kernels, on_device(): pl.pallas_call(place, out_shape=tuple((jax.ShapeDtypeStruct(own.shape, f3...  1.82 us

profile of v6, /device:TPU:0, one launch (start us, length us, event | category | flops | bytes accessed | tf_op | source)
XLA Modules:
  0.0 44.8 jit_solution(1651460176230220113)
XLA Ops:
  0.6 42.4 %inversion.1 = (f32[2,64,512]{2,1,0:T(8,128)}, f32[2,512]{1,0:T(2,128)}, f32[2,64,512]{2,1,0:T(8,128)}, f32[2,64]{1,0:T(2,128)}) custom-call(bf16[64,256]{1,0:T(8,128)(2,1)} %bitcast.3, f32[16,256]{1,0:T(8,128)} %obs_hbm.1, bf16[2,128,256]{2,1,0:T(8,128)(2,1)} %bitcast.2, f32[2,64,512]{2,1,0:T(8,128)} %w_in_hbm.1, f32[2,512]{1,0:T(2,128)} %b_in_hbm.1, ...), custom_call_target="tpu_custom_call" | custom-call | tf_op jit(solution)/shard_map/inversion/pallas_call | solution.py:395
  43.0 1.8 %place.1 = (f32[2,64,512]{2,1,0:T(8,128)}, f32[2,512]{1,0:T(2,128)}, f32[2,64,512]{2,1,0:T(8,128)}, f32[2,64]{1,0:T(2,128)}) custom-call(f32[2,64,512]{2,1,0:T(8,128)} %get-tuple-element.8.refs_0_, f32[2,512]{1,0:T(2,128)} %get-tuple-element.9.refs_1_, f32[2,64,512]{2,1,0:T(8,128)} %get-tuple-element.10.refs_2_, f32[2,64]{1,0:T(2,128)} %get-tuple-element.11.refs_3_), custom_call_target="tpu_custom_call" | custom-call | tf_op jit(solution)/shard_map/place/pallas_call | solution.py:436

commit v7 on v6

--- a/solution.py
+++ b/solution.py
@@ -122,9 +122,14 @@
     def pass_on(src, sem, target):
         send(src, src, code_send.at[sem], code_recv.at[sem], (target, places[0]))
 
-    pass_on(code.at[m], 0, p_at[0] + 1 - q)
+    cut = per // 2
+    first_half, second_half = pl.ds(0, cut), pl.ds(cut, per - cut)
+    pass_on(code.at[m, first_half], 0, p_at[0] + 1 - q)
     for t in range(1, pairs):
-        pass_on(code.at[m], t, p_at[t] + q)
+        pass_on(code.at[m, second_half], t, p_at[t] + q)
+    pass_on(code.at[m, second_half], pairs, p_at[0] + 1 - q)
+    for t in range(1, pairs):
+        pass_on(code.at[m, first_half], pairs + t, p_at[t] + q)
 
     lane = lax.broadcasted_iota(jnp.int32, (K, 128), 1)
     row = lax.broadcasted_iota(jnp.int32, (K, 128), 0)
@@ -138,21 +143,20 @@
         hidden = jnp.tanh(pre.astype(bf16))
         return jnp.dot(weights[j, A:rows, :], hidden, preferred_element_type=f32)
 
-    cut = per // 2
-    first_half, second_half = pl.ds(0, cut), pl.ds(cut, per - cut)
-
     def forward():
         for t in range(pairs):
-            settle(code.at[0], code_recv.at[t])
+            settle(code.at[0, second_half if t else first_half], code_recv.at[t])
         for t in range(1, pairs):
-            pass_on(code.at[p_at[0] + 1 - q, first_half], pairs + t, p_at[t] + q)
+            pass_on(code.at[p_at[0] + 1 - q, first_half], 2 * pairs + t, p_at[t] + q)
         for t in range(1, pairs):
-            pass_on(code.at[p_at[t] + q, second_half], 2 * pairs + t, p_at[0] + 1 - q)
+            pass_on(code.at[p_at[t] + q, second_half], 3 * pairs + t, p_at[0] + 1 - q)
 
     def decode():
+        for t in range(pairs):
+            settle(code.at[0, first_half if t else second_half], code_recv.at[pairs + t])
         for t in range(1, pairs):
-            settle(code.at[0, first_half], code_recv.at[pairs + t])
-            settle(code.at[0, second_half], code_recv.at[2 * pairs + t])
+            settle(code.at[0, first_half], code_recv.at[2 * pairs + t])
+            settle(code.at[0, second_half], code_recv.at[3 * pairs + t])
 
         def chunk(i, carry):
             slot = lax.rem(m + 1 + i // (per * (rows // 16)), M)
@@ -358,10 +362,11 @@
     for t in range(1, Z):
         settle(xg.at[0, pl.ds(0, F)], x_send.at[t])
     for t in range(pairs):
-        settle(code.at[0], code_send.at[t])
+        settle(code.at[0, second_half if t else first_half], code_send.at[t])
+        settle(code.at[0, first_half if t else second_half], code_send.at[pairs + t])
     for t in range(1, pairs):
-        settle(code.at[0, first_half], code_send.at[pairs + t])
-        settle(code.at[0, second_half], code_send.at[2 * pairs + t])
+        settle(code.at[0, first_half], code_send.at[2 * pairs + t])
+        settle(code.at[0, second_half], code_send.at[3 * pairs + t])
     for update in range(UPDATES):
         settle(fresh, w_send.at[update])
         settle(got.at[update, pl.ds(0, slots - 1)], piece_send.at[update])

time: 45 us -> 45 us (level)
  no operation moved by 1% of the time
where the time goes in v7:
time: 45 us; the launch traced here: 44.8 us
  Pallas kernels  44.2 us (98%)
  between operations  0.64 us (1%)
    pallas_call x1, Pallas kernels, on_device(): pl.pallas_call(functools.partial(kernel, M, Z, total), out_shape=tuple((j...  42.4 us
    pallas_call x1, Pallas kernels, on_device(): pl.pallas_call(place, out_shape=tuple((jax.ShapeDtypeStruct(own.shape, f3...  1.82 us

profile of v7, /device:TPU:0, one launch (start us, length us, event | category | flops | bytes accessed | tf_op | source)
XLA Modules:
  0.0 44.8 jit_solution(8793924502711581422)
XLA Ops:
  0.6 42.4 %inversion.1 = (f32[2,64,512]{2,1,0:T(8,128)}, f32[2,512]{1,0:T(2,128)}, f32[2,64,512]{2,1,0:T(8,128)}, f32[2,64]{1,0:T(2,128)}) custom-call(bf16[64,256]{1,0:T(8,128)(2,1)} %bitcast.3, f32[16,256]{1,0:T(8,128)} %obs_hbm.1, bf16[2,128,256]{2,1,0:T(8,128)(2,1)} %bitcast.2, f32[2,64,512]{2,1,0:T(8,128)} %w_in_hbm.1, f32[2,512]{1,0:T(2,128)} %b_in_hbm.1, ...), custom_call_target="tpu_custom_call" | custom-call | tf_op jit(solution)/shard_map/inversion/pallas_call | solution.py:400
  43.0 1.8 %place.1 = (f32[2,64,512]{2,1,0:T(8,128)}, f32[2,512]{1,0:T(2,128)}, f32[2,64,512]{2,1,0:T(8,128)}, f32[2,64]{1,0:T(2,128)}) custom-call(f32[2,64,512]{2,1,0:T(8,128)} %get-tuple-element.8.refs_0_, f32[2,512]{1,0:T(2,128)} %get-tuple-element.9.refs_1_, f32[2,64,512]{2,1,0:T(8,128)} %get-tuple-element.10.refs_2_, f32[2,64]{1,0:T(2,128)} %get-tuple-element.11.refs_3_), custom_call_target="tpu_custom_call" | custom-call | tf_op jit(solution)/shard_map/place/pallas_call | solution.py:441
